TPU v7x, 32 devices: a whole 2x2x4 slice. The times are simulated.
32 devices in a mesh: dp: 16 (over z, y, x), tensor: 2 (over core).
Axes of the slice: x: 2, y: 2, z: 4, core: 2. Of those that a mesh axis runs over, the one named last changes fastest.
Arguments:
- images: bfloat16 [16, 584, 1024], P('dp'), may hold values from -6 to 6
- image_mask: int32 [16], P('dp'), may hold values 0 or 1
- cotangent: bfloat16 [16, 584, 1024], P('dp'), may hold values from -6 to 6
- ln1_gain: bfloat16 [1024], replicated, may hold values from 0.5 to 1.5
- ln1_bias: bfloat16 [1024], replicated, may hold values from -1.25 to 1.25
- w_qkv: bfloat16 [1024, 3, 1024], P(None, None, 'tensor'), may hold values from -0.1875 to 0.1875
- qv_bias: bfloat16 [2, 1024], P(None, 'tensor'), may hold values from -1.75 to 1.75
- w_out: bfloat16 [1024, 1024], P('tensor'), may hold values from -3 to 3
- out_bias: bfloat16 [1024], replicated, may hold values from -1.75 to 1.75
- ln2_gain: bfloat16 [1024], replicated, may hold values from 0.5 to 1.5
- ln2_bias: bfloat16 [1024], replicated, may hold values from -1.25 to 1.25
- w_up: bfloat16 [1024, 4096], P(None, 'tensor'), may hold values from -0.1875 to 0.1875
- up_bias: bfloat16 [4096], P('tensor'), may hold values from -1.75 to 1.75
- w_down: bfloat16 [4096, 1024], P('tensor'), may hold values from -0.09375 to 0.09375
- down_bias: bfloat16 [1024], replicated, may hold values from -1.75 to 1.75
Outputs:
- block_output: bfloat16 [16, 584, 1024], P('dp')
- images_grad: bfloat16 [16, 584, 1024], P('dp')
- ln1_gain_grad: float32 [1024], replicated
- ln1_bias_grad: float32 [1024], replicated
- w_qkv_grad: float32 [1024, 3, 1024], P(None, None, 'tensor')
- qv_bias_grad: float32 [2, 1024], P(None, 'tensor')
- w_out_grad: float32 [1024, 1024], P('tensor')
- out_bias_grad: float32 [1024], replicated
- ln2_gain_grad: float32 [1024], replicated
- ln2_bias_grad: float32 [1024], replicated
- w_up_grad: float32 [1024, 4096], P(None, 'tensor')
- up_bias_grad: float32 [4096], P('tensor')
- w_down_grad: float32 [4096, 1024], P('tensor')
- down_bias_grad: float32 [1024], replicated
All inputs are finite; a program needn't handle non-finite values. No bound on the sum of `image_mask` on one device may be relied on, other than what follows from the above.
Results may differ from a plain program's by a relative error of at most 0.017.
Values may be sent and summed in bfloat16 or wider, within the bound.
No kernel may reach another device: no remote copies, remote signals or barrier semaphores. Data moves between devices by JAX's collectives and lax.ppermute only.
A program may use at most 192 MiB of HBM per device.

v0:
```python
import jax
import jax.numpy as jnp
from jax import lax
from jax.sharding import PartitionSpec as P

HD = 64
VALID = 577


eps_norm = 1e-06


def normalize(values, gain, shift):
    mean = jnp.mean(values, axis=-1, keepdims=True)
    centred = values - mean
    spread = jnp.mean(centred * centred, axis=-1, keepdims=True)
    return centred * lax.rsqrt(spread + eps_norm) * gain + shift


def inner_rows(left, right):
    return lax.dot_general(
        left, right, (((0,), (0,)), ((), ())), preferred_element_type=jnp.float32
    )


def times_back(left, weight):
    return lax.dot_general(
        left, weight, (((1,), (1,)), ((), ())), preferred_element_type=jnp.float32
    )


def score_block(query, keyset):
    raw = jnp.einsum("qhd,khd->hqk", query, keyset, preferred_element_type=jnp.float32)
    live = jnp.arange(raw.shape[-1]) < VALID
    return jnp.where(live, raw * HD ** (-0.5), -1e30)


def attend_forward(inputs):
    query, keyset, valueset = inputs
    scores = score_block(query, keyset)
    peak = jnp.max(scores, axis=-1, keepdims=True)
    expo = jnp.exp(scores - peak)
    total = jnp.sum(expo, axis=-1, keepdims=True)
    probs = (expo / total).astype(jnp.bfloat16)
    mixed = jnp.einsum("hqk,khd->qhd", probs, valueset, preferred_element_type=jnp.float32)
    return (mixed.astype(jnp.bfloat16), peak[..., 0] + jnp.log(total[..., 0]))


def attend_backward(inputs):
    query, keyset, valueset, grad_mixed, logsum = inputs
    scores = score_block(query, keyset)
    probs = jnp.exp(scores - logsum[..., None])
    grad_probs = jnp.einsum(
        "qhd,khd->hqk", grad_mixed, valueset, preferred_element_type=jnp.float32
    )
    delta = jnp.sum(probs * grad_probs, axis=-1, keepdims=True)
    grad_scores = (probs * (grad_probs - delta) * HD ** (-0.5)).astype(jnp.bfloat16)
    low_probs = probs.astype(jnp.bfloat16)
    grad_value = jnp.einsum(
        "hqk,qhd->khd", low_probs, grad_mixed, preferred_element_type=jnp.float32
    )
    grad_query = jnp.einsum("hqk,khd->qhd", grad_scores, keyset, preferred_element_type=jnp.float32)
    grad_key = jnp.einsum("hqk,qhd->khd", grad_scores, query, preferred_element_type=jnp.float32)
    return jnp.stack([grad_query, grad_key, grad_value], axis=1).astype(jnp.bfloat16)


def shards(
    images,
    image_mask,
    cotangent,
    ln1_gain,
    ln1_bias,
    w_qkv,
    qv_bias,
    w_out,
    out_bias,
    ln2_gain,
    ln2_bias,
    w_up,
    up_bias,
    w_down,
    down_bias,
):
    count, seq, width = images.shape
    total_rows = count * seq
    parts = lax.axis_size("tensor")
    share = total_rows // parts
    begin = lax.axis_index("tensor") * share
    local = w_qkv.shape[2]
    heads_local = local // HD
    gain1 = ln1_gain.astype(jnp.float32)
    shift1 = ln1_bias.astype(jnp.float32)
    gain2 = ln2_gain.astype(jnp.float32)
    shift2 = ln2_bias.astype(jnp.float32)
    inputs = images.reshape(total_rows, width).astype(jnp.float32)
    normed1 = normalize(inputs, gain1, shift1).astype(jnp.bfloat16)
    w_qkv_flat = w_qkv.reshape(width, 3 * local)
    bias_row = jnp.concatenate([qv_bias[0], jnp.zeros_like(qv_bias[0]), qv_bias[1]]).astype(
        jnp.float32
    )
    qkv = (jnp.dot(normed1, w_qkv_flat, preferred_element_type=jnp.float32) + bias_row).astype(
        jnp.bfloat16
    )
    split = qkv.reshape(count, seq, 3, heads_local, HD)
    queries = split[:, :, 0]
    keys_all = split[:, :, 1]
    values_all = split[:, :, 2]
    mixed, logsums = lax.map(attend_forward, (queries, keys_all, values_all))
    mixed_rows = mixed.reshape(total_rows, local)
    attn_part = lax.psum_scatter(
        jnp.dot(mixed_rows, w_out, preferred_element_type=jnp.float32),
        "tensor",
        scatter_dimension=0,
        tiled=True,
    )
    input_rows = lax.dynamic_slice_in_dim(inputs, begin, share, 0)
    resid = input_rows + attn_part + out_bias.astype(jnp.float32)
    normed2 = normalize(resid, gain2, shift2).astype(jnp.bfloat16)
    gathered = lax.all_gather(normed2, "tensor", axis=0, tiled=True)
    pre = jnp.dot(gathered, w_up, preferred_element_type=jnp.float32) + up_bias.astype(jnp.float32)
    act, gelu_back = jax.vjp(lambda v: jax.nn.gelu(v, approximate=False), pre)
    act_low = act.astype(jnp.bfloat16)
    mlp_part = lax.psum_scatter(
        jnp.dot(act_low, w_down, preferred_element_type=jnp.float32).astype(jnp.bfloat16),
        "tensor",
        scatter_dimension=0,
        tiled=True,
    ).astype(jnp.float32)
    result_rows = (resid + mlp_part + down_bias.astype(jnp.float32)).astype(jnp.bfloat16)
    block_output = lax.all_gather(result_rows, "tensor", axis=0, tiled=True).reshape(
        count, seq, width
    )
    keep = image_mask.astype(jnp.bfloat16)[:, None, None]
    grad_out = (cotangent * keep).reshape(total_rows, width)
    grad_wdown = inner_rows(act_low, grad_out)
    grad_bdown = jnp.sum(grad_out.astype(jnp.float32), axis=0)
    grad_act = times_back(grad_out, w_down)
    grad_pre = gelu_back(grad_act)[0].astype(jnp.bfloat16)
    grad_wup = inner_rows(gathered, grad_pre)
    grad_bup = jnp.sum(grad_pre.astype(jnp.float32), axis=0)
    grad_normed2 = lax.psum_scatter(
        times_back(grad_pre, w_up), "tensor", scatter_dimension=0, tiled=True
    )
    own_grad_out = lax.dynamic_slice_in_dim(grad_out, begin, share, 0)
    norm2_value, norm2_back = jax.vjp(normalize, resid, gain2, shift2)
    grad_resid_part, grad_gain2, grad_shift2 = norm2_back(grad_normed2)
    grad_resid = own_grad_out.astype(jnp.float32) + grad_resid_part
    grad_bout = jnp.sum(grad_resid, axis=0)
    resid_all = lax.all_gather(grad_resid.astype(jnp.bfloat16), "tensor", axis=0, tiled=True)
    grad_wout = inner_rows(mixed_rows, resid_all)
    grad_mixed = (
        times_back(resid_all, w_out).astype(jnp.bfloat16).reshape(count, seq, heads_local, HD)
    )
    grad_split = lax.map(attend_backward, (queries, keys_all, values_all, grad_mixed, logsums))
    grad_qkv = grad_split.reshape(total_rows, 3 * local)
    grad_wqkv = inner_rows(normed1, grad_qkv).reshape(width, 3, local)
    bias_sums = jnp.sum(grad_qkv.astype(jnp.float32), axis=0).reshape(3, local)
    grad_qvb = jnp.stack([bias_sums[0], bias_sums[2]])
    grad_normed1 = lax.psum_scatter(
        times_back(grad_qkv, w_qkv_flat), "tensor", scatter_dimension=0, tiled=True
    )
    norm1_value, norm1_back = jax.vjp(normalize, input_rows, gain1, shift1)
    grad_input_part, grad_gain1, grad_shift1 = norm1_back(grad_normed1)
    grad_rows = (grad_resid + grad_input_part).astype(jnp.bfloat16)
    images_grad = lax.all_gather(grad_rows, "tensor", axis=0, tiled=True).reshape(count, seq, width)
    summed_gain1, summed_shift1, summed_bout, summed_gain2, summed_shift2 = lax.psum(
        (grad_gain1, grad_shift1, grad_bout, grad_gain2, grad_shift2), ("dp", "tensor")
    )
    summed_wqkv, summed_qvb, summed_wout, summed_wup, summed_bup, summed_wdown, summed_bdown = (
        lax.psum(grad_wqkv.astype(jnp.bfloat16), "dp").astype(jnp.float32),
        lax.psum(grad_qvb.astype(jnp.bfloat16), "dp").astype(jnp.float32),
        lax.psum(grad_wout.astype(jnp.bfloat16), "dp").astype(jnp.float32),
        lax.psum(grad_wup.astype(jnp.bfloat16), "dp").astype(jnp.float32),
        lax.psum(grad_bup.astype(jnp.bfloat16), "dp").astype(jnp.float32),
        lax.psum(grad_wdown.astype(jnp.bfloat16), "dp").astype(jnp.float32),
        lax.psum(grad_bdown.astype(jnp.bfloat16), "dp").astype(jnp.float32),
    )
    return (
        block_output,
        images_grad,
        summed_gain1,
        summed_shift1,
        summed_wqkv,
        summed_qvb,
        summed_wout,
        summed_bout,
        summed_gain2,
        summed_shift2,
        summed_wup,
        summed_bup,
        summed_wdown,
        summed_bdown,
    )


def solution(mesh):
    in_specs = (
        P("dp", None, None),
        P("dp"),
        P("dp", None, None),
        P(),
        P(),
        P(None, None, "tensor"),
        P(None, "tensor"),
        P("tensor", None),
        P(),
        P(),
        P(),
        P(None, "tensor"),
        P("tensor"),
        P("tensor", None),
        P(),
    )
    out_specs = (
        P("dp", None, None),
        P("dp", None, None),
        P(),
        P(),
        P(None, None, "tensor"),
        P(None, "tensor"),
        P("tensor", None),
        P(),
        P(),
        P(),
        P(None, "tensor"),
        P("tensor"),
        P("tensor", None),
        P(),
    )
    return jax.shard_map(shards, mesh=mesh, in_specs=in_specs, out_specs=out_specs, check_vma=False)
```

profile of v0, /device:TPU:0, one launch (start us, length us, event | category | flops | bytes accessed | tf_op | source)
XLA Modules:
  0.0 655.7 jit_solution(7852224685704166118)
XLA Ops:
  12.1 4.7 copy.46
  17.5 5.4 add_convert_fusion.1
  37.9 6.4 fusion
  50.9 5.1 concatenate.14
  63.2 9.1 %all-gather.9.cloned.1.call-done = bf16[2,292,1024]{2,1,0:T(8,128)(2,1)} async-done(((bf16[1,292,1024]{2,1,0:T(8,128)(2,1)}), bf16[2,292,1024]{2,1,0:T(8,128)(2,1)}) %all-gather.9.cloned.1.call-update) | async-done | bytes 1196048 | tf_op jit(solution)/shard_map/all_gather | solution.py:119
  74.8 14.6 %multiply_convert_fusion.1 = (bf16[584,2048]{1,0:T(8,128)(2,1)S(1)}, f32[584,2048]{1,0:T(8,128)S(1)}, f32[584,2048]{1,0:T(8,128)S(1)}) fusion(f32[2048]{0:T(1024)S(1)} %convert_element_type.174, bf16[584,1024]{1,0:T(8,128)(2,1)} %reshape.249, bf16[1024,2048]{1,0:T(8,128)(2,1)} %param.26), kind=kOutput, calls=%fused_computation.27 | convolution fusion | flops 2528411648 | bytes 17358848 | tf_op jit(solution)/shard_map/dot_general | solution.py:120
  93.1 5.0 fusion.93
  103.7 6.3 fusion.2
  112.8 5.5 fusion.1
  122.6 4.9 concatenate.15
  139.5 9.8 %all-gather.13.cloned.1.call-done = bf16[2,292,1024]{2,1,0:T(8,128)(2,1)} async-done(((bf16[1,292,1024]{2,1,0:T(8,128)(2,1)}), bf16[2,292,1024]{2,1,0:T(8,128)(2,1)}) %all-gather.13.cloned.1.call-update) | async-done | bytes 1196048 | tf_op jit(solution)/shard_map/all_gather | solution.py:149
  157.1 7.6 %fusion.66 = f32[8,584,584]{1,2,0:T(8,128)} fusion(bf16[584,8,64]{0,2,1:T(8,128)(2,1)} %bitcast.129, bf16[1,584,3,8,64]{1,4,3,2,0:T(8,128)(2,1)S(1)} %bitcast.124), kind=kOutput, calls=%fused_computation.89 | convolution fusion | flops 349241344 | bytes 12167168 | tf_op jit(solution)/shard_map/while/body/eval_jaxpr/qhd,khd->hqk/dot_general | solution.py:53
  164.6 22.5 %fusion.48 = bf16[584,1,8,64]{0,3,2,1:T(8,128)(2,1)} fusion(f32[8,584,584]{1,2,0:T(8,128)} %fusion.66, f32[8,584,584]{1,2,0:T(8,128)} %copy-done.1, f32[8,584]{1,0:T(8,128)S(1)} %log_add_fusion, pred[584]{0:T(1024)(128)(4,1)S(1)} %copy-done.47, bf16[1,584,3,8,64]{1,4,3,2,0:T(8,128)(2,1)S(1)} %bitcast.125), kind=kOutput, calls=%fused_computation.56 | convolution fusion | flops 379259520 | bytes 49137664 | tf_op jit(solution)/shard_map/while/body/eval_jaxpr/hqk,khd->qhd/dot_general | solution.py:62
  187.2 22.3 %fusion.51 = bf16[584,1,8,64]{0,3,2,1:T(8,128)(2,1)} fusion(f32[8,584,584]{1,2,0:T(8,128)} %fusion.66, f32[8,584,584]{1,2,0:T(8,128)} %copy-done.1, f32[8,584]{1,0:T(8,128)S(1)} %log_add_fusion, pred[584]{0:T(1024)(128)(4,1)S(1)} %copy-done.47, bf16[1,584,3,8,64]{1,4,3,2,0:T(8,128)(2,1)S(1)} %bitcast.126), kind=kOutput, calls=%fused_computation.57 | convolution fusion | flops 379259520 | bytes 49137664 | tf_op jit(solution)/shard_map/while/body/eval_jaxpr/hqk,qhd->khd/dot_general | solution.py:63
  209.5 7.5 %fusion.45 = bf16[584,1,8,64]{0,3,2,1:T(8,128)(2,1)S(1)} fusion(bf16[584,8,64]{0,2,1:T(8,128)(2,1)} %bitcast.130, f32[8,584,584]{1,2,0:T(8,128)} %copy-done.1, f32[8,584]{1,0:T(8,128)S(1)} %log_add_fusion, pred[584]{0:T(1024)(128)(4,1)S(1)} %copy-done.47), kind=kOutput, calls=%fused_computation.55 | convolution fusion | flops 360155136 | bytes 12129096 | tf_op jit(solution)/shard_map/while/body/eval_jaxpr/hqk,qhd->khd/dot_general | solution.py:59
  223.1 6.4 fusion.3
  232.2 6.7 %convolution_convert_fusion.1 = bf16[1024,2048]{1,0:T(8,128)(2,1)} fusion(bf16[584,1024]{1,0:T(8,128)(2,1)S(1)} %copy-done.23, bf16[584,2048]{1,0:T(8,128)(2,1)} %copy-done.55), kind=kOutput, calls=%fused_computation.43 | convolution fusion | flops 2451570688 | bytes 7782400 | tf_op jit(solution)/shard_map/dot_general | solution.py:21
  238.9 5.2 concatenate.17
  249.6 6.9 %convolution_convert_fusion = bf16[2048,1024]{1,0:T(8,128)(2,1)} fusion(bf16[584,2048]{1,0:T(8,128)(2,1)} %copy-done.56, bf16[1,584,1024]{2,1,0:T(8,128)(2,1)S(1)} %copy-done.15), kind=kOutput, calls=%fused_computation.42 | convolution fusion | flops 2451570688 | bytes 7782400 | tf_op jit(solution)/shard_map/dot_general | solution.py:21
  258.8 4.8 convolution_convert_fusion.2
  264.3 44.8 %all-reduce.9 = (bf16[2,512]{1,0:T(2,128)(2,1)S(1)}, bf16[2048]{0:T(1024)(128)(2,1)S(1)}, bf16[1024]{0:T(1024)(128)(2,1)S(1)}) all-reduce(bf16[2,512]{1,0:T(2,128)(2,1)S(1)} %pad_maximum_fusion, bf16[2048]{0:T(1024)(128)(2,1)S(1)} %copy-done.45, bf16[1024]{0:T(1024)(128)(2,1)S(1)} %copy-done.39), channel_id=1, replica_groups=mesh['dp'=16,'tensor'=2] {'dp'}, use_global_device_ids=true, to_apply=%region_23.24 | all-reduce | flops 4096 | bytes 16384 | tf_op jit(solution)/shard_map/psum | solution.py:171
  313.6 41.8 %all-reduce.8 = (f32[1024]{0:T(1024)}, f32[1024]{0:T(1024)}, f32[1024]{0:T(1024)}, f32[1024]{0:T(1024)}, f32[1024]{0:T(1024)}) all-reduce(f32[1024]{0:T(1024)S(1)} %get-tuple-element.53, f32[1024]{0:T(1024)S(1)} %get-tuple-element.58, f32[1024]{0:T(1024)S(1)} %get-tuple-element.85, ...), channel_id=1, replica_groups=mesh['dp'=16,'tensor'=2] {'dp','tensor'}, use_global_device_ids=true, to_apply=%region_18.19 | all-reduce | flops 5120 | bytes 40960 | tf_op jit(solution)/shard_map/psum | solution.py:166
  357.9 274.4 %all-reduce.13.cloned.1.call-done = (bf16[1024,3,512]{2,0,1:T(8,128)(2,1)}, bf16[512,1024]{1,0:T(8,128)(2,1)}, bf16[1024,2048]{1,0:T(8,128)(2,1)}, bf16[2048,1024]{1,0:T(8,128)(2,1)}) async-done(((bf16[1024,3,512]{2,0,1:T(8,128)(2,1)}, bf16[512,1024]{1,0:T(8,128)(2,1)}, bf16[1024,2048]{1,0:T(8,128)(2,1)}, bf16[2048,1024]{1,0:T(8,128)(2,1)}), (bf16[1024,3,512]{2,0,1:T(8,128)(2,1)}, ...) | async-done | bytes 12582928 | tf_op jit(solution)/shard_map/psum | solution.py:170
  632.3 6.8 %convert_element_type.198 = f32[1024,2048]{1,0:T(8,128)} convert(bf16[1024,2048]{1,0:T(8,128)(2,1)} %get-tuple-element.71) | non-fusion elementwise | flops 2097152 | bytes 12582912 | tf_op jit(solution)/shard_map/convert_element_type | solution.py:173
  (202 shorter events, 104.8 us)
Async XLA Ops:
  7.2 29.9 %copy-start = (bf16[512,1024]{1,0:T(8,128)(2,1)S(1)}, bf16[512,1024]{1,0:T(8,128)(2,1)}, u32[]{:S(2)}) copy-start(bf16[512,1024]{1,0:T(8,128)(2,1)} %param.22) | copy-start | bytes 3145732
  7.2 65.0 %all-gather.9.cloned.1.call-start = ((), (), s32[]{:S(2)}) async-start(), calls=%async_computation | async-start | bytes 1818624 | tf_op jit(solution)/shard_map/all_gather | solution.py:119
  7.3 23.8 %copy-start.46 = (pred[584]{0:T(1024)(128)(4,1)}, pred[584]{0:T(1024)(128)(4,1)S(1)}, u32[]{:S(2)}) copy-start(pred[584]{0:T(1024)(128)(4,1)S(1)} %iota_compare_fusion) | copy-start | bytes 1756
  8.9 8.0 %copy-start.37 = (f32[584]{0:T(1024)}, f32[584]{0:T(1024)S(1)}, u32[]{:S(2)}) copy-start(f32[584]{0:T(1024)S(1)} %broadcast_multiply_fusion.1) | copy-start | bytes 7012
  45.1 5.8 collective-permute-start
  49.3 9.7 %copy-start.30 = (f32[292]{0:T(512)}, f32[292]{0:T(512)S(1)}, u32[]{:S(2)}) copy-start(f32[292]{0:T(512)S(1)} %broadcast_multiply_fusion.2) | copy-start | bytes 3508
  60.2 89.1 %all-gather.13.cloned.1.call-start = ((), (), s32[]{:S(2)}) async-start(), calls=%async_computation.2 | async-start | bytes 1818624 | tf_op jit(solution)/shard_map/all_gather | solution.py:149
  63.2 29.9 %copy-start.12 = (bf16[1,584,1024]{2,1,0:T(8,128)(2,1)}, bf16[1,584,1024]{2,1,0:T(8,128)(2,1)S(1)}, u32[]{:S(2)}) copy-start(bf16[1,584,1024]{2,1,0:T(8,128)(2,1)S(1)} %get-tuple-element.74) | copy-start | bytes 3588100
  74.8 14.7 %copy-start.53 = (bf16[2048,1024]{1,0:T(8,128)(2,1)S(1)}, bf16[2048,1024]{1,0:T(8,128)(2,1)}, u32[]{:S(2)}) copy-start(bf16[2048,1024]{1,0:T(8,128)(2,1)} %param.28) | copy-start | bytes 12582916
  110.0 17.5 %copy-start.10 = (f32[296,1024]{1,0:T(8,128)}, f32[296,1024]{1,0:T(8,128)S(1)}, u32[]{:S(2)}) copy-start(f32[296,1024]{1,0:T(8,128)S(1)} %fusion.2) | copy-start | bytes 3637252
  110.0 17.5 %collective-permute-start.2 = (f32[4,1024]{1,0:T(4,128)S(1)}, f32[4,1024]{1,0:T(4,128)}, u32[]{:S(2)}, u32[]{:S(2)}) collective-permute-start(f32[4,1024]{1,0:T(4,128)S(1)} %slice.47), channel_id=1, source_target_pairs={{0,1},{2,3},{4,5},{6,7},{8,9},{10,11},{12,13},{14,15},{16,17},{18,... | collective-permute-start | bytes 49160
  119.1 3.6 collective-permute-start.1
  138.7 172.2 %all-gather.11.cloned.1.call-start = ((), (), s32[]{:S(2)}) async-start(), calls=%async_computation.1 | async-start | bytes 1818624 | tf_op jit(solution)/shard_map/all_gather | solution.py:130
  139.5 215.9 %all-gather.15.cloned.1.call-start = ((), (), s32[]{:S(2)}) async-start(), calls=%async_computation.3 | async-start | bytes 1818624 | tf_op jit(solution)/shard_map/all_gather | solution.py:165
  157.1 7.6 %copy-start.47 = (pred[584]{0:T(1024)(128)(4,1)S(1)}, pred[584]{0:T(1024)(128)(4,1)}, u32[]{:S(2)}) copy-start(pred[584]{0:T(1024)(128)(4,1)} %copy-done.46) | copy-start | bytes 1756
  209.5 7.5 %copy-start.26 = (bf16[584,1,8,64]{0,3,2,1:T(8,128)(2,1)S(1)}, bf16[584,1,8,64]{0,3,2,1:T(8,128)(2,1)}, u32[]{:S(2)}) copy-start(bf16[584,1,8,64]{0,3,2,1:T(8,128)(2,1)} %fusion.48) | copy-start | bytes 1794052
  209.5 7.5 %copy-start.27 = (bf16[584,1,8,64]{0,3,2,1:T(8,128)(2,1)S(1)}, bf16[584,1,8,64]{0,3,2,1:T(8,128)(2,1)}, u32[]{:S(2)}) copy-start(bf16[584,1,8,64]{0,3,2,1:T(8,128)(2,1)} %fusion.51) | copy-start | bytes 1794052
  223.1 9.1 %copy-start.23 = (bf16[584,1024]{1,0:T(8,128)(2,1)S(1)}, bf16[584,1024]{1,0:T(8,128)(2,1)}, u32[]{:S(2)}) copy-start(bf16[584,1024]{1,0:T(8,128)(2,1)} %reshape.249) | copy-start | bytes 3588100
  229.6 14.6 %copy-start.29 = (f32[1024]{0:T(1024)S(1)}, f32[1024]{0:T(1024)}, u32[]{:S(2)}) copy-start(f32[1024]{0:T(1024)} %copy-done.28) | copy-start | bytes 12292
  229.6 14.5 %copy-start.31 = (f32[292]{0:T(512)S(1)}, f32[292]{0:T(512)}, u32[]{:S(2)}) copy-start(f32[292]{0:T(512)} %copy-done.30) | copy-start | bytes 3508
  229.6 9.3 %collective-permute-start.3 = (f32[4,1024]{1,0:T(4,128)S(1)}, f32[4,1024]{1,0:T(4,128)S(1)}, u32[]{:S(2)}, u32[]{:S(2)}) collective-permute-start(f32[4,1024]{1,0:T(4,128)S(1)} %slice.48), channel_id=1, source_target_pairs={{0,1},{2,3},{4,5},{6,7},{8,9},{10,11},{12,13},{14,15},{16,17},{18,... | collective-permute-start | bytes 49160
  249.5 382.8 %all-reduce.13.cloned.1.call-start = ((), (), s32[]{:S(2)}) async-start(), calls=%async_computation.4 | async-start | bytes 25165824 | tf_op jit(solution)/shard_map/psum | solution.py:170
  263.6 49.9 %copy-start.35 = (f32[1024]{0:T(1024)S(1)}, f32[1024]{0:T(1024)}, u32[]{:S(2)}) copy-start(f32[1024]{0:T(1024)} %get-tuple-element.55) | copy-start | bytes 12292
  263.6 49.9 %copy-start.36 = (f32[1024]{0:T(1024)S(1)}, f32[1024]{0:T(1024)}, u32[]{:S(2)}) copy-start(f32[1024]{0:T(1024)} %get-tuple-element.57) | copy-start | bytes 12292
  (42 other events, 161.7 us)
Sparse Core Ops, SparseCore 0:
  60.3 11.8 all-gather.8
  138.8 10.4 all-gather.12
  150.9 10.4 all-gather.10
  249.6 10.4 all-gather.14
  267.5 364.7 all-reduce.12
where the time goes:
time: 666 us; the launch traced here: 656 us
  waiting for transfers between devices  293 us (44%)
  matrix products  127 us (19%)
  blocking collectives  111 us (17%)
  local copies, waits for them, and re-layouts  51.2 us (8%)
  other arithmetic  46.7 us (7%)
  between operations  16.3 us (2%)
  starting transfers between devices  10.2 us (2%)
    psum x1, waiting for transfers between devices, shards(): lax.psum(grad_wqkv.astype(jnp.bfloat16), 'dp').astype(jnp.float32)  274 us
    psum x1, blocking collectives, shards(): lax.psum(grad_qvb.astype(jnp.bfloat16), 'dp').astype(jnp.float32)  44.8 us
    psum x1, blocking collectives, shards(): lax.psum((grad_gain1, grad_shift1, grad_bout, grad_gain2, grad_shift2), (...  41.8 us
    unnamed x126, local copies, waits for them, and re-layouts  40.2 us
    unnamed x4, blocking collectives  24.6 us
    dot_general x1, matrix products, attend_backward(): jnp.einsum('hqk,khd->qhd', grad_scores, keyset, preferred_element_type=jn...  22.5 us
    dot_general x1, matrix products, attend_backward(): jnp.einsum('hqk,qhd->khd', grad_scores, query, preferred_element_type=jnp...  22.3 us
    dot_general x4, matrix products, inner_rows(): lax.dot_general(left, right, (((0,), (0,)), ((), ())), preferred_element_...  20.3 us
  transfers between devices with their start and end apart: 9, of which 3 were waited for; matrix products, arithmetic and copies ran while one was open for 20% of the time, Pallas kernels for 0%

commit v1 on v0

v1 whole, which is shorter than its diff:
```python
import jax
import jax.numpy as jnp
from jax import lax
from jax.sharding import PartitionSpec as P

HD = 64
VALID = 577
EPS = 1e-06
BF = jnp.bfloat16
F32 = jnp.float32


def stats(values):
    mean = jnp.mean(values, axis=-1, keepdims=True)
    centred = values - mean
    spread = jnp.mean(centred * centred, axis=-1, keepdims=True)
    inv = lax.rsqrt(spread + EPS)
    return centred * inv, inv


def norm_back(unit, inv, gain, grad):
    scaled = grad * gain
    mean_a = jnp.mean(scaled, axis=-1, keepdims=True)
    mean_b = jnp.mean(scaled * unit, axis=-1, keepdims=True)
    return inv * (scaled - mean_a - unit * mean_b)


def inner_rows(left, right):
    return lax.dot_general(
        left, right, (((0,), (0,)), ((), ())), preferred_element_type=F32
    )


def times_back(left, weight):
    return lax.dot_general(
        left, weight, (((1,), (1,)), ((), ())), preferred_element_type=F32
    )


def score_block(query, keyset):
    raw = jnp.einsum("qhd,khd->hqk", query, keyset, preferred_element_type=F32)
    live = jnp.arange(raw.shape[-1]) < VALID
    return jnp.where(live, raw * HD ** (-0.5), -1e30)


def attend_forward(query, keyset, valueset):
    scores = score_block(query, keyset)
    peak = jnp.max(scores, axis=-1, keepdims=True)
    expo = jnp.exp(scores - peak)
    total = jnp.sum(expo, axis=-1, keepdims=True)
    probs = (expo / total).astype(BF)
    mixed = jnp.einsum("hqk,khd->qhd", probs, valueset, preferred_element_type=F32)
    return mixed.astype(BF), peak[..., 0] + jnp.log(total[..., 0])


def attend_backward(query, keyset, valueset, grad_mixed, logsum):
    scores = score_block(query, keyset)
    probs = jnp.exp(scores - logsum[..., None])
    grad_probs = jnp.einsum("qhd,khd->hqk", grad_mixed, valueset, preferred_element_type=F32)
    delta = jnp.sum(probs * grad_probs, axis=-1, keepdims=True)
    grad_scores = (probs * (grad_probs - delta) * HD ** (-0.5)).astype(BF)
    low_probs = probs.astype(BF)
    grad_value = jnp.einsum("hqk,qhd->khd", low_probs, grad_mixed, preferred_element_type=F32)
    grad_query = jnp.einsum("hqk,khd->qhd", grad_scores, keyset, preferred_element_type=F32)
    grad_key = jnp.einsum("hqk,qhd->khd", grad_scores, query, preferred_element_type=F32)
    return jnp.stack([grad_query, grad_key, grad_value], axis=1).astype(BF)


def swap_sum(part):
    if lax.axis_size("tensor") == 2:
        other = lax.ppermute(part, "tensor", [(0, 1), (1, 0)])
        return part.astype(F32) + other.astype(F32)
    return lax.psum(part.astype(F32), "tensor")


def xor_pairs(bit):
    return [(i, i ^ bit) for i in range(lax.axis_size("dp"))]


def bits_of():
    count = lax.axis_size("dp")
    bits = []
    while count > 1:
        if count % 2:
            raise ValueError("dp")
        bits.append(1 << len(bits))
        count //= 2
    return bits


def sum_small(vector):
    for bit in bits_of():
        vector = vector + lax.ppermute(vector, "dp", xor_pairs(bit))
    return vector


def cut_thirds(rows, turn):
    unit = 128
    whole = rows // unit
    base = whole // 3
    counts = [base + (1 if (i - turn) % 3 < whole % 3 else 0) for i in range(3)]
    return [c * unit for c in counts]


def sum_over_dp(matrix, turn):
    bits = bits_of()
    index = lax.axis_index("dp")
    halving = bits[: min(3, len(bits) - 1)]
    swaps = bits[len(halving) :]
    pieces, orders, start = [], [], 0
    for lane, rows in enumerate(cut_thirds(matrix.shape[0], turn)):
        if rows == 0:
            continue
        pieces.append(lax.slice_in_dim(matrix, start, start + rows, axis=0))
        turned = lane % len(halving)
        orders.append(halving[turned:] + halving[:turned])
        start += rows
    for step in range(len(halving)):
        for lane in range(len(pieces)):
            piece, bit = pieces[lane], orders[lane][step]
            half = piece.shape[0] // 2
            side = (index // bit) & 1
            kept = lax.dynamic_slice_in_dim(piece, side * half, half, 0)
            sent = lax.dynamic_slice_in_dim(piece, (1 - side) * half, half, 0)
            pieces[lane] = kept + lax.ppermute(sent, "dp", xor_pairs(bit))
    for bit in swaps:
        for lane in range(len(pieces)):
            pieces[lane] = pieces[lane] + lax.ppermute(pieces[lane], "dp", xor_pairs(bit))
    for step in reversed(range(len(halving))):
        for lane in range(len(pieces)):
            piece, bit = pieces[lane], orders[lane][step]
            other = lax.ppermute(piece, "dp", xor_pairs(bit))
            side = (index // bit) & 1
            pieces[lane] = jnp.where(
                side == 0,
                jnp.concatenate([piece, other], axis=0),
                jnp.concatenate([other, piece], axis=0),
            )
    return jnp.concatenate(pieces, axis=0).astype(F32)


def shards(
    images,
    image_mask,
    cotangent,
    ln1_gain,
    ln1_bias,
    w_qkv,
    qv_bias,
    w_out,
    out_bias,
    ln2_gain,
    ln2_bias,
    w_up,
    up_bias,
    w_down,
    down_bias,
):
    count, seq, width = images.shape
    rows = count * seq
    local = w_qkv.shape[2]
    heads = local // HD
    gain1 = ln1_gain.astype(F32)
    gain2 = ln2_gain.astype(F32)
    inputs = images.reshape(rows, width).astype(F32)
    keep = image_mask.astype(BF)[:, None, None]
    grad_out = (cotangent * keep).reshape(rows, width)
    w_qkv_flat = w_qkv.reshape(width, 3 * local)
    bias_row = jnp.concatenate([qv_bias[0], jnp.zeros_like(qv_bias[0]), qv_bias[1]]).astype(F32)

    unit1, inv1 = stats(inputs)
    normed1 = (unit1 * gain1 + ln1_bias.astype(F32)).astype(BF)
    qkv = (jnp.dot(normed1, w_qkv_flat, preferred_element_type=F32) + bias_row).astype(BF)
    split = qkv.reshape(count, seq, 3, heads, HD)
    attended = [attend_forward(split[i, :, 0], split[i, :, 1], split[i, :, 2]) for i in range(count)]
    mixed = jnp.concatenate([a[0] for a in attended], axis=0).reshape(rows, local)
    attn = swap_sum(jnp.dot(mixed, w_out, preferred_element_type=F32).astype(BF))
    grad_act = times_back(grad_out, w_down)
    resid = inputs + attn + out_bias.astype(F32)
    unit2, inv2 = stats(resid)
    normed2 = (unit2 * gain2 + ln2_bias.astype(F32)).astype(BF)
    pre = jnp.dot(normed2, w_up, preferred_element_type=F32) + up_bias.astype(F32)
    cdf = 0.5 * (1.0 + lax.erf(pre * (0.5**0.5)))
    act = (pre * cdf).astype(BF)
    slope = cdf + pre * jnp.exp(-0.5 * pre * pre) * ((0.5 / jnp.pi) ** 0.5)
    grad_pre = (grad_act * slope).astype(BF)
    grad_wdown = inner_rows(act, grad_out).astype(BF)
    summed_wdown = sum_over_dp(grad_wdown, 0)
    grad_wup = inner_rows(normed2, grad_pre).astype(BF)
    summed_wup = sum_over_dp(grad_wup, 1)
    grad_normed2 = swap_sum(times_back(grad_pre, w_up).astype(BF))
    mlp = swap_sum(jnp.dot(act, w_down, preferred_element_type=F32).astype(BF))
    block_output = (resid + mlp + down_bias.astype(F32)).astype(BF).reshape(images.shape)
    grad_resid = grad_out.astype(F32) + norm_back(unit2, inv2, gain2, grad_normed2)
    resid_low = grad_resid.astype(BF)
    grad_wout = inner_rows(mixed, resid_low).astype(BF)
    summed_wout = sum_over_dp(grad_wout, 2)
    grad_mixed = times_back(resid_low, w_out).astype(BF).reshape(count, seq, heads, HD)
    grad_qkv = jnp.concatenate(
        [
            attend_backward(split[i, :, 0], split[i, :, 1], split[i, :, 2], grad_mixed[i], attended[i][1])
            for i in range(count)
        ],
        axis=0,
    ).reshape(rows, 3 * local)
    grad_wqkv = inner_rows(normed1, grad_qkv).astype(BF)
    summed_wqkv = sum_over_dp(grad_wqkv, 0).reshape(width, 3, local)
    bias_sums = jnp.sum(grad_qkv.astype(F32), axis=0)
    grad_normed1 = swap_sum(times_back(grad_qkv, w_qkv_flat).astype(BF))
    images_grad = (
        (grad_resid + norm_back(unit1, inv1, gain1, grad_normed1)).astype(BF).reshape(images.shape)
    )

    small = [
        jnp.sum(grad_normed1 * unit1, axis=0),
        jnp.sum(grad_normed1, axis=0),
        jnp.sum(grad_resid, axis=0),
        jnp.sum(grad_normed2 * unit2, axis=0),
        jnp.sum(grad_normed2, axis=0),
        jnp.sum(grad_out.astype(F32), axis=0),
        jnp.sum(grad_pre.astype(F32), axis=0),
        bias_sums[:local],
        bias_sums[2 * local :],
    ]
    flat = jnp.concatenate(small)
    length = flat.shape[0]
    padded = -(-length // 1024) * 1024
    flat = sum_small(jnp.pad(flat, (0, padded - length)).reshape(padded // 128, 128)).reshape(-1)
    out, at = [], 0
    for part in small:
        out.append(flat[at : at + part.shape[0]])
        at += part.shape[0]
    return (
        block_output,
        images_grad,
        out[0],
        out[1],
        summed_wqkv,
        jnp.stack([out[7], out[8]]),
        summed_wout,
        out[2],
        out[3],
        out[4],
        summed_wup,
        out[6],
        summed_wdown,
        out[5],
    )


def solution(mesh):
    in_specs = (
        P("dp", None, None),
        P("dp"),
        P("dp", None, None),
        P(),
        P(),
        P(None, None, "tensor"),
        P(None, "tensor"),
        P("tensor", None),
        P(),
        P(),
        P(),
        P(None, "tensor"),
        P("tensor"),
        P("tensor", None),
        P(),
    )
    out_specs = (
        P("dp", None, None),
        P("dp", None, None),
        P(),
        P(),
        P(None, None, "tensor"),
        P(None, "tensor"),
        P("tensor", None),
        P(),
        P(),
        P(),
        P(None, "tensor"),
        P("tensor"),
        P("tensor", None),
        P(),
    )
    return jax.shard_map(shards, mesh=mesh, in_specs=in_specs, out_specs=out_specs, check_vma=False)
```

time: 666 us -> 574 us (0.86)
  blocking collectives: 111 us -> 0 us
  waiting for transfers between devices: 293 us -> 185 us
  starting transfers between devices: 10.2 us -> 107 us
  other arithmetic: 46.7 us -> 110 us
  matrix products: 127 us -> 109 us
  between operations: 16.3 us -> 3.29 us
    psum x1 -> x0, waiting for transfers between devices: 274 us -> none  [shards(): lax.psum(grad_wqkv.astype(jnp.bfloat16), 'dp').astype(jnp.float32)]
    ppermute x0 -> x92, waiting for transfers between devices: none -> 185 us  [the longest x36 109 us: sum_over_dp(): pieces[lane] = kept + lax.ppermute(sent, 'dp', xor_pairs(bit))]
    ppermute x0 -> x92, starting transfers between devices: none -> 107 us  [the longest x36 43.1 us: sum_over_dp(): pieces[lane] = kept + lax.ppermute(sent, 'dp', xor_pairs(bit))]
    psum x2 -> x0, blocking collectives: 86.6 us -> none  [the longest x1 44.8 us: shards(): lax.psum(grad_qvb.astype(jnp.bfloat16), 'dp').astype(jnp.float32)]
    select_n x0 -> x42, other arithmetic: none -> 58.6 us  [sum_over_dp(): jnp.where(side == 0, jnp.concatenate([piece, other], axis=0), jnp.concate...]
    unnamed x126 -> x158, local copies, waits for them, and re-layouts: 40.2 us -> 14.4 us
    unnamed x4 -> x0, blocking collectives: 24.6 us -> none
    all_gather x4 -> x0, waiting for transfers between devices: 18.9 us -> none  [the longest x1 9.81 us: shards(): lax.all_gather(grad_resid.astype(jnp.bfloat16), 'tensor', axis=0, tiled=T...]
  transfers between devices with their start and end apart: 9 -> 92, of which waited for: 3 -> 39; matrix products, arithmetic and copies ran while one was open for 20% -> 36% of each run, Pallas kernels for 0% -> 0%
where the time goes in v1:
time: 574 us; the launch traced here: 569 us
  waiting for transfers between devices  185 us (32%)
  other arithmetic  110 us (19%)
  matrix products  109 us (19%)
  starting transfers between devices  107 us (19%)
  local copies, waits for them, and re-layouts  55.6 us (10%)
    ppermute x36, waiting for transfers between devices, sum_over_dp(): pieces[lane] = kept + lax.ppermute(sent, 'dp', xor_pairs(bit))  109 us
    select_n x42, other arithmetic, sum_over_dp(): jnp.where(side == 0, jnp.concatenate([piece, other], axis=0), jnp.concate...  58.6 us
    ppermute x36, waiting for transfers between devices, sum_over_dp(): other = lax.ppermute(piece, 'dp', xor_pairs(bit))  54.8 us
    ppermute x36, starting transfers between devices, sum_over_dp(): pieces[lane] = kept + lax.ppermute(sent, 'dp', xor_pairs(bit))  43.1 us
    ppermute x36, starting transfers between devices, sum_over_dp(): other = lax.ppermute(piece, 'dp', xor_pairs(bit))  39 us
    dot_general x1, matrix products, attend_backward(): jnp.einsum('hqk,khd->qhd', grad_scores, keyset, preferred_element_type=F32)  22.9 us
    dot_general x1, matrix products, attend_backward(): jnp.einsum('hqk,qhd->khd', grad_scores, query, preferred_element_type=F32)  22.6 us
    ppermute x12, starting transfers between devices, sum_over_dp(): lax.ppermute(pieces[lane], 'dp', xor_pairs(bit))  18.9 us
  transfers between devices with their start and end apart: 92, of which 39 were waited for; matrix products, arithmetic and copies ran while one was open for 36% of the time, Pallas kernels for 0%

profile of v1, /device:TPU:0, one launch (start us, length us, event | category | flops | bytes accessed | tf_op | source)
XLA Modules:
  0.0 569.1 jit_solution(12127885679682259867)
XLA Ops:
  0.7 4.8 copy.62
  6.3 5.5 add_convert_fusion
  24.3 4.5 fusion.73
  39.0 5.5 convert_reduce_fusion
  54.4 4.2 convolution_convert_fusion.1
  65.0 11.5 %collective-permute-done.50 = bf16[128,2048]{1,0:T(8,128)(2,1)S(1)} collective-permute-done((bf16[128,2048]{1,0:T(8,128)(2,1)S(1)}, bf16[128,2048]{1,0:T(8,128)(2,1)S(1)}, u32[]{:S(2)}, u32[]{:S(2)}) %collective-permute-start.50) | collective-permute-done | bytes 524320 | tf_op jit(solution)/shard_map/ppermute | solution.py:125
  78.1 16.4 %collective-permute-done.85 = bf16[320,1024]{1,0:T(8,128)(2,1)S(1)} collective-permute-done((bf16[320,1024]{1,0:T(8,128)(2,1)S(1)}, bf16[320,1024]{1,0:T(8,128)(2,1)S(1)}, u32[]{:S(2)}, u32[]{:S(2)}) %collective-permute-start.85) | collective-permute-done | bytes 655392 | tf_op jit(solution)/shard_map/ppermute | solution.py:125
  99.2 20.0 %collective-permute-done.51 = bf16[64,2048]{1,0:T(8,128)(2,1)S(1)} collective-permute-done((bf16[64,2048]{1,0:T(8,128)(2,1)S(1)}, bf16[64,2048]{1,0:T(8,128)(2,1)S(1)}, u32[]{:S(2)}, u32[]{:S(2)}) %collective-permute-start.51) | collective-permute-done | bytes 262176 | tf_op jit(solution)/shard_map/ppermute | solution.py:125
  123.6 7.8 %collective-permute-done.52 = bf16[32,2048]{1,0:T(8,128)(2,1)S(1)} collective-permute-done((bf16[32,2048]{1,0:T(8,128)(2,1)S(1)}, bf16[32,2048]{1,0:T(8,128)(2,1)S(1)}, u32[]{:S(2)}, u32[]{:S(2)}) %collective-permute-start.52) | collective-permute-done | bytes 131104 | tf_op jit(solution)/shard_map/ppermute | solution.py:125
  171.2 7.5 %fusion.94 = f32[8,584,584]{1,2,0:T(8,128)} fusion(bf16[584,8,64]{0,2,1:T(8,128)(2,1)S(1)} %bitcast.135, bf16[1,584,3,8,64]{1,4,3,2,0:T(8,128)(2,1)} %bitcast.130), kind=kOutput, calls=%fused_computation.134 | convolution fusion | flops 349241344 | bytes 12167168 | tf_op jit(solution)/shard_map/qhd,khd->hqk/dot_general | solution.py:59
  178.7 8.1 %fusion.80 = bf16[584,1,8,64]{0,3,2,1:T(8,128)(2,1)} fusion(bf16[584,8,64]{0,2,1:T(8,128)(2,1)S(1)} %bitcast.136, f32[8,584,584]{1,2,0:T(8,128)} %copy-done.2, f32[8,584]{1,0:T(8,128)S(1)} %log_add_fusion, pred[584]{0:T(1024)(128)(4,1)S(1)} %copy-done.65), kind=kOutput, calls=%fused_computation.100 | convolution fusion | flops 360454144 | bytes 12129096 | tf_op jit(solution)/shard_map/hqk,qhd->khd/dot_general | solution.py:63
  186.8 22.6 %fusion.74 = bf16[584,1,8,64]{0,3,2,1:T(8,128)(2,1)} fusion(f32[8,584,584]{1,2,0:T(8,128)} %fusion.94, f32[8,584,584]{1,2,0:T(8,128)} %copy-done.2, f32[8,584]{1,0:T(8,128)S(1)} %log_add_fusion, pred[584]{0:T(1024)(128)(4,1)S(1)} %copy-done.65, bf16[1,584,3,8,64]{1,4,3,2,0:T(8,128)(2,1)} %bitcast.131), kind=kOutput, calls=%fused_computation.98 | convolution fusion | flops 379558528 | bytes 49137664 | tf_op jit(solution)/shard_map/hqk,qhd->khd/dot_general | solution.py:65
  209.4 22.9 %fusion.77 = bf16[584,1,8,64]{0,3,2,1:T(8,128)(2,1)} fusion(f32[8,584,584]{1,2,0:T(8,128)} %fusion.94, f32[8,584,584]{1,2,0:T(8,128)} %copy-done.2, f32[8,584]{1,0:T(8,128)S(1)} %log_add_fusion, pred[584]{0:T(1024)(128)(4,1)S(1)} %copy-done.65, bf16[1,584,3,8,64]{1,4,3,2,0:T(8,128)(2,1)} %bitcast.132), kind=kOutput, calls=%fused_computation.99 | convolution fusion | flops 379558528 | bytes 49137664 | tf_op jit(solution)/shard_map/hqk,khd->qhd/dot_general | solution.py:64
  237.7 4.3 convolution_convert_fusion
  292.2 4.4 collective-permute-done.39
  305.1 4.3 collective-permute-done.33
  309.4 4.2 collective-permute-done.41
  327.1 11.1 %collective-permute-done.45 = bf16[32,1024]{1,0:T(8,128)(2,1)S(1)} collective-permute-done((bf16[32,1024]{1,0:T(8,128)(2,1)S(1)}, bf16[32,1024]{1,0:T(8,128)(2,1)S(1)}, u32[]{:S(2)}, u32[]{:S(2)}) %collective-permute-start.45) | collective-permute-done | bytes 65568 | tf_op jit(solution)/shard_map/ppermute | solution.py:125
  343.5 4.3 collective-permute-done.46
  352.7 24.0 %collective-permute-done.61 = bf16[48,2048]{1,0:T(8,128)(2,1)S(1)} collective-permute-done((bf16[48,2048]{1,0:T(8,128)(2,1)S(1)}, bf16[48,2048]{1,0:T(8,128)(2,1)S(1)}, u32[]{:S(2)}, u32[]{:S(2)}) %collective-permute-start.61) | collective-permute-done | bytes 196640 | tf_op jit(solution)/shard_map/ppermute | solution.py:132
  380.5 7.0 %collective-permute-done.23 = bf16[64,1536]{1,0:T(8,128)(2,1)S(1)} collective-permute-done((bf16[64,1536]{1,0:T(8,128)(2,1)S(1)}, bf16[64,1536]{1,0:T(8,128)(2,1)S(1)}, u32[]{:S(2)}, u32[]{:S(2)}) %collective-permute-start.23) | collective-permute-done | bytes 196640 | tf_op jit(solution)/shard_map/ppermute | solution.py:125
  411.1 4.8 collective-permute-done.25
  419.8 5.9 %collective-permute-done.26 = bf16[32,1536]{1,0:T(8,128)(2,1)S(1)} collective-permute-done((bf16[32,1536]{1,0:T(8,128)(2,1)S(1)}, bf16[32,1536]{1,0:T(8,128)(2,1)S(1)}, u32[]{:S(2)}, u32[]{:S(2)}) %collective-permute-start.26) | collective-permute-done | bytes 98336 | tf_op jit(solution)/shard_map/ppermute | solution.py:132
  564.2 4.6 copy.72
  (530 shorter events, 345.9 us)
Async XLA Ops:
  59.0 102.4 %collective-permute-start.2 = (bf16[584,1024]{1,0:T(8,128)(2,1)S(1)}, bf16[584,1024]{1,0:T(8,128)(2,1)S(1)}, u32[]{:S(2)}, u32[]{:S(2)}) collective-permute-start(bf16[584,1024]{1,0:T(8,128)(2,1)S(1)} %convolution_convert_fusion.3), channel_id=1, source_target_pairs={{0,1},{1,0},{2,3},{3,2},{4,5},{5,4},{6,7},{7,6},{8,9},{9,8},{10,11... | collective-permute-start | bytes 3588104 | tf_op jit(solution)/shard_map/ppermute | solution.py:71
  59.4 105.2 %collective-permute-start.1 = (bf16[584,1024]{1,0:T(8,128)(2,1)S(1)}, bf16[584,1024]{1,0:T(8,128)(2,1)S(1)}, u32[]{:S(2)}, u32[]{:S(2)}) collective-permute-start(bf16[584,1024]{1,0:T(8,128)(2,1)S(1)} %convolution_convert_fusion.4), channel_id=1, source_target_pairs={{0,1},{1,0},{2,3},{3,2},{4,5},{5,4},{6,7},{7,6},{8,9},{9,8},{10,11... | collective-permute-start | bytes 3588104 | tf_op jit(solution)/shard_map/ppermute | solution.py:71
  59.6 38.7 %collective-permute-start.64 = (bf16[192,2048]{1,0:T(8,128)(2,1)S(1)}, bf16[192,2048]{1,0:T(8,128)(2,1)S(1)}, u32[]{:S(2)}, u32[]{:S(2)}) collective-permute-start(bf16[192,2048]{1,0:T(8,128)(2,1)S(1)} %constant_dynamic-slice_fusion.11), channel_id=1, source_target_pairs={{0,8},{2,10},{4,12},{6,14},{8,0},{10,2},{12,4},{14,6},{16,24},{18,... | collective-permute-start | bytes 2359304 | tf_op jit(solution)/shard_map/ppermute | solution.py:125
  64.3 30.2 %collective-permute-start.85 = (bf16[320,1024]{1,0:T(8,128)(2,1)S(1)}, bf16[320,1024]{1,0:T(8,128)(2,1)S(1)}, u32[]{:S(2)}, u32[]{:S(2)}) collective-permute-start(bf16[320,1024]{1,0:T(8,128)(2,1)S(1)} %constant_dynamic-slice_fusion.2), channel_id=1, source_target_pairs={{0,8},{2,10},{4,12},{6,14},{8,0},{10,2},{12,4},{14,6},{16,24},{18,... | collective-permute-start | bytes 1966088 | tf_op jit(solution)/shard_map/ppermute | solution.py:125
  153.2 98.9 %collective-permute-start.88 = (bf16[80,1024]{1,0:T(8,128)(2,1)}, bf16[80,1024]{1,0:T(8,128)(2,1)}, u32[]{:S(2)}, u32[]{:S(2)}) collective-permute-start(bf16[80,1024]{1,0:T(8,128)(2,1)} %dynamic-slice_add_fusion.22), channel_id=1, source_target_pairs={{0,16},{2,18},{4,20},{6,22},{8,24},{10,26},{12,28},{14,30},{16,0},... | collective-permute-start | bytes 491528 | tf_op jit(solution)/shard_map/ppermute | solution.py:128
  157.5 96.8 %collective-permute-start.81 = (bf16[80,1024]{1,0:T(8,128)(2,1)}, bf16[80,1024]{1,0:T(8,128)(2,1)}, u32[]{:S(2)}, u32[]{:S(2)}) collective-permute-start(bf16[80,1024]{1,0:T(8,128)(2,1)} %dynamic-slice_add_fusion.23), channel_id=1, source_target_pairs={{0,16},{2,18},{4,20},{6,22},{8,24},{10,26},{12,28},{14,30},{16,0},... | collective-permute-start | bytes 491528 | tf_op jit(solution)/shard_map/ppermute | solution.py:128
  159.0 105.0 %collective-permute-start.66 = (bf16[48,2048]{1,0:T(8,128)(2,1)}, bf16[48,2048]{1,0:T(8,128)(2,1)}, u32[]{:S(2)}, u32[]{:S(2)}) collective-permute-start(bf16[48,2048]{1,0:T(8,128)(2,1)} %constant_dynamic-slice_fusion.9), channel_id=1, source_target_pairs={{0,4},{2,6},{4,0},{6,2},{8,12},{10,14},{12,8},{14,10},{16,20},{18,... | collective-permute-start | bytes 589832 | tf_op jit(solution)/shard_map/ppermute | solution.py:125
  161.3 105.2 %collective-permute-start.59 = (bf16[48,2048]{1,0:T(8,128)(2,1)}, bf16[48,2048]{1,0:T(8,128)(2,1)}, u32[]{:S(2)}, u32[]{:S(2)}) collective-permute-start(bf16[48,2048]{1,0:T(8,128)(2,1)} %constant_dynamic-slice_fusion.12), channel_id=1, source_target_pairs={{0,2},{2,0},{4,6},{6,4},{8,10},{10,8},{12,14},{14,12},{16,18},{18,... | collective-permute-start | bytes 589832 | tf_op jit(solution)/shard_map/ppermute | solution.py:125
  254.2 34.7 %collective-permute-start.55 = (bf16[64,2048]{1,0:T(8,128)(2,1)}, bf16[64,2048]{1,0:T(8,128)(2,1)S(1)}, u32[]{:S(2)}, u32[]{:S(2)}) collective-permute-start(bf16[64,2048]{1,0:T(8,128)(2,1)} %maximum_select_fusion.35), channel_id=1, source_target_pairs={{0,4},{2,6},{4,0},{6,2},{8,12},{10,14},{12,8},{14,10},{16,20},{18,... | collective-permute-start | bytes 786440 | tf_op jit(solution)/shard_map/ppermute | solution.py:132
  264.1 35.6 %collective-permute-start.89 = (bf16[80,1024]{1,0:T(8,128)(2,1)S(1)}, bf16[80,1024]{1,0:T(8,128)(2,1)S(1)}, u32[]{:S(2)}, u32[]{:S(2)}) collective-permute-start(bf16[80,1024]{1,0:T(8,128)(2,1)S(1)} %add.558), channel_id=1, source_target_pairs={{0,4},{2,6},{4,0},{6,2},{8,12},{10,14},{12,8},{14,10},{16,20},{18,... | collective-permute-start | bytes 491528 | tf_op jit(solution)/shard_map/ppermute | solution.py:132
  266.5 34.4 %collective-permute-start.82 = (bf16[80,1024]{1,0:T(8,128)(2,1)S(1)}, bf16[80,1024]{1,0:T(8,128)(2,1)S(1)}, u32[]{:S(2)}, u32[]{:S(2)}) collective-permute-start(bf16[80,1024]{1,0:T(8,128)(2,1)S(1)} %add.548), channel_id=1, source_target_pairs={{0,2},{2,0},{4,6},{6,4},{8,10},{10,8},{12,14},{14,12},{16,18},{18,... | collective-permute-start | bytes 491528 | tf_op jit(solution)/shard_map/ppermute | solution.py:132
  285.1 32.9 %collective-permute-start.67 = (bf16[48,2048]{1,0:T(8,128)(2,1)S(1)}, bf16[48,2048]{1,0:T(8,128)(2,1)S(1)}, u32[]{:S(2)}, u32[]{:S(2)}) collective-permute-start(bf16[48,2048]{1,0:T(8,128)(2,1)S(1)} %dynamic-slice_add_fusion.19), channel_id=1, source_target_pairs={{0,16},{2,18},{4,20},{6,22},{8,24},{10,26},{12,28},{14,30},{16,0},... | collective-permute-start | bytes 589832 | tf_op jit(solution)/shard_map/ppermute | solution.py:128
  318.0 159.1 %collective-permute-start.3 = (bf16[584,1024]{1,0:T(8,128)(2,1)}, bf16[584,1024]{1,0:T(8,128)(2,1)}, u32[]{:S(2)}, u32[]{:S(2)}) collective-permute-start(bf16[584,1024]{1,0:T(8,128)(2,1)} %convolution_convert_fusion.6), channel_id=1, source_target_pairs={{0,1},{1,0},{2,3},{3,2},{4,5},{5,4},{6,7},{7,6},{8,9},{9,8},{10,11... | collective-permute-start | bytes 3588104 | tf_op jit(solution)/shard_map/ppermute | solution.py:71
  318.1 60.5 %collective-permute-start.15 = (bf16[192,1536]{1,0:T(8,128)(2,1)S(1)}, bf16[192,1536]{1,0:T(8,128)(2,1)S(1)}, u32[]{:S(2)}, u32[]{:S(2)}) collective-permute-start(bf16[192,1536]{1,0:T(8,128)(2,1)S(1)} %copy-done.50), channel_id=1, source_target_pairs={{0,4},{2,6},{4,0},{6,2},{8,12},{10,14},{12,8},{14,10},{16,20},{18,... | collective-permute-start | bytes 1769480 | tf_op jit(solution)/shard_map/ppermute | solution.py:125
  347.8 42.0 %collective-permute-start.8 = (bf16[192,1536]{1,0:T(8,128)(2,1)S(1)}, bf16[192,1536]{1,0:T(8,128)(2,1)S(1)}, u32[]{:S(2)}, u32[]{:S(2)}) collective-permute-start(bf16[192,1536]{1,0:T(8,128)(2,1)S(1)} %copy-done.49), channel_id=1, source_target_pairs={{0,2},{2,0},{4,6},{6,4},{8,10},{10,8},{12,14},{14,12},{16,18},{18,... | collective-permute-start | bytes 1769480 | tf_op jit(solution)/shard_map/ppermute | solution.py:125
  348.9 61.4 %collective-permute-start.56 = (bf16[128,2048]{1,0:T(8,128)(2,1)S(1)}, bf16[128,2048]{1,0:T(8,128)(2,1)S(1)}, u32[]{:S(2)}, u32[]{:S(2)}) collective-permute-start(bf16[128,2048]{1,0:T(8,128)(2,1)S(1)} %maximum_select_fusion.20), channel_id=1, source_target_pairs={{0,2},{2,0},{4,6},{6,4},{8,10},{10,8},{12,14},{14,12},{16,18},{18,... | collective-permute-start | bytes 1572872 | tf_op jit(solution)/shard_map/ppermute | solution.py:132
  394.1 42.1 %collective-permute-start.69 = (bf16[96,2048]{1,0:T(8,128)(2,1)}, bf16[96,2048]{1,0:T(8,128)(2,1)}, u32[]{:S(2)}, u32[]{:S(2)}) collective-permute-start(bf16[96,2048]{1,0:T(8,128)(2,1)} %maximum_select_fusion.25), channel_id=1, source_target_pairs={{0,2},{2,0},{4,6},{6,4},{8,10},{10,8},{12,14},{14,12},{16,18},{18,... | collective-permute-start | bytes 1179656 | tf_op jit(solution)/shard_map/ppermute | solution.py:132
  395.6 47.4 %collective-permute-start.62 = (bf16[96,2048]{1,0:T(8,128)(2,1)}, bf16[96,2048]{1,0:T(8,128)(2,1)}, u32[]{:S(2)}, u32[]{:S(2)}) collective-permute-start(bf16[96,2048]{1,0:T(8,128)(2,1)} %maximum_select_fusion.24), channel_id=1, source_target_pairs={{0,8},{2,10},{4,12},{6,14},{8,0},{10,2},{12,4},{14,6},{16,24},{18,... | collective-permute-start | bytes 1179656 | tf_op jit(solution)/shard_map/ppermute | solution.py:132
  427.2 59.3 %collective-permute-start.91 = (bf16[320,1024]{1,0:T(8,128)(2,1)}, bf16[320,1024]{1,0:T(8,128)(2,1)}, u32[]{:S(2)}, u32[]{:S(2)}) collective-permute-start(bf16[320,1024]{1,0:T(8,128)(2,1)} %maximum_select_fusion.15), channel_id=1, source_target_pairs={{0,8},{2,10},{4,12},{6,14},{8,0},{10,2},{12,4},{14,6},{16,24},{18,... | collective-permute-start | bytes 1966088 | tf_op jit(solution)/shard_map/ppermute | solution.py:132
  436.2 55.2 %collective-permute-start.84 = (bf16[320,1024]{1,0:T(8,128)(2,1)}, bf16[320,1024]{1,0:T(8,128)(2,1)}, u32[]{:S(2)}, u32[]{:S(2)}) collective-permute-start(bf16[320,1024]{1,0:T(8,128)(2,1)} %maximum_select_fusion.14), channel_id=1, source_target_pairs={{0,4},{2,6},{4,0},{6,2},{8,12},{10,14},{12,8},{14,10},{16,20},{18,... | collective-permute-start | bytes 1966088 | tf_op jit(solution)/shard_map/ppermute | solution.py:132
  467.9 68.5 %collective-permute-start.70 = (bf16[192,2048]{1,0:T(8,128)(2,1)}, bf16[192,2048]{1,0:T(8,128)(2,1)}, u32[]{:S(2)}, u32[]{:S(2)}) collective-permute-start(bf16[192,2048]{1,0:T(8,128)(2,1)} %maximum_select_fusion.12), channel_id=1, source_target_pairs={{0,8},{2,10},{4,12},{6,14},{8,0},{10,2},{12,4},{14,6},{16,24},{18,... | collective-permute-start | bytes 2359304 | tf_op jit(solution)/shard_map/ppermute | solution.py:132
  473.2 65.3 %collective-permute-start.63 = (bf16[192,2048]{1,0:T(8,128)(2,1)}, bf16[192,2048]{1,0:T(8,128)(2,1)}, u32[]{:S(2)}, u32[]{:S(2)}) collective-permute-start(bf16[192,2048]{1,0:T(8,128)(2,1)} %maximum_select_fusion.11), channel_id=1, source_target_pairs={{0,4},{2,6},{4,0},{6,2},{8,12},{10,14},{12,8},{14,10},{16,20},{18,... | collective-permute-start | bytes 2359304 | tf_op jit(solution)/shard_map/ppermute | solution.py:132
  485.2 59.4 %collective-permute-start.77 = (bf16[384,1024]{1,0:T(8,128)(2,1)}, bf16[384,1024]{1,0:T(8,128)(2,1)}, u32[]{:S(2)}, u32[]{:S(2)}) collective-permute-start(bf16[384,1024]{1,0:T(8,128)(2,1)} %maximum_select_fusion.13), channel_id=1, source_target_pairs={{0,2},{2,0},{4,6},{6,4},{8,10},{10,8},{12,14},{14,12},{16,18},{18,... | collective-permute-start | bytes 2359304 | tf_op jit(solution)/shard_map/ppermute | solution.py:132
  525.4 31.0 %collective-permute-start.14 = (bf16[192,1536]{1,0:T(8,128)(2,1)}, bf16[192,1536]{1,0:T(8,128)(2,1)}, u32[]{:S(2)}, u32[]{:S(2)}) collective-permute-start(bf16[192,1536]{1,0:T(8,128)(2,1)} %maximum_select_fusion.16), channel_id=1, source_target_pairs={{0,2},{2,0},{4,6},{6,4},{8,10},{10,8},{12,14},{14,12},{16,18},{18,... | collective-permute-start | bytes 1769480 | tf_op jit(solution)/shard_map/ppermute | solution.py:132
  (142 other events, 1560.6 us)

commit v2 on v1

--- a/solution.py
+++ b/solution.py
@@ -1,6 +1,8 @@
 import jax
 import jax.numpy as jnp
 from jax import lax
+from jax.experimental import pallas as pl
+from jax.experimental.pallas import tpu as pltpu
 from jax.sharding import PartitionSpec as P
 
 HD = 64
@@ -139,7 +141,7 @@
     return jnp.concatenate(pieces, axis=0).astype(F32)
 
 
-def shards(
+def shards_any(
     images,
     image_mask,
     cotangent,
@@ -248,6 +250,801 @@
     )
 
 
+ANY = pl.BlockSpec(memory_space=pl.ANY)
+VM = pl.BlockSpec(memory_space=pltpu.VMEM)
+SM = pl.BlockSpec(memory_space=pltpu.SMEM)
+MIB = 1024 * 1024
+
+
+def shape_of(shape, dtype):
+    return jax.ShapeDtypeStruct(shape, dtype)
+
+
+def nn(left, right):
+    return jnp.dot(left, right, preferred_element_type=F32)
+
+
+def normal_unit(values):
+    mean = jnp.mean(values, axis=-1, keepdims=True)
+    centred = values - mean
+    spread = jnp.mean(centred * centred, axis=-1, keepdims=True)
+    inv = lax.rsqrt(spread + EPS)
+    return centred * inv, inv
+
+
+def call(body, args, in_specs, outs, out_specs, scratch=(), grid=(), vmem=40, aliases=None, name=None, prefetch=0):
+    spec = pltpu.PrefetchScalarGridSpec(
+        num_scalar_prefetch=prefetch,
+        grid=grid,
+        in_specs=in_specs,
+        out_specs=out_specs,
+        scratch_shapes=list(scratch),
+    )
+    return pl.pallas_call(
+        body,
+        out_shape=outs,
+        grid_spec=spec,
+        input_output_aliases=aliases or {},
+        compiler_params=pltpu.CompilerParams(vmem_limit_bytes=vmem * MIB),
+        name=name,
+    )(*args)
+
+
+def row_chunks(rows):
+    units, parts = rows // 16, 4
+    cuts = [16 * (units * i // parts) for i in range(parts)] + [rows]
+    return [(cuts[i], cuts[i + 1] - cuts[i]) for i in range(parts)]
+
+
+def lane_halves():
+    return lax.broadcasted_iota(jnp.int32, (1, 2 * HD), 1) < HD
+
+
+def key_mask(length):
+    return jnp.where(lax.broadcasted_iota(jnp.int32, (1, length), 1) < VALID, 0.0, -1e30)
+
+
+def attend_kernel(
+    x_ref, vec_ref, bias_ref, w_ref, wo_ref, part_ref, q_ref, k_ref, v_ref, mixed_ref, n1_ref, lse_ref, w_buf, sems
+):
+    rows, width = x_ref.shape
+    padded = q_ref.shape[0]
+    local = q_ref.shape[1]
+    copies = [pltpu.make_async_copy(w_ref.at[c], w_buf.at[c], sems.at[c]) for c in range(3)]
+    for copy in copies:
+        copy.start()
+    unit, _ = normal_unit(x_ref[...].astype(F32))
+    normed = unit * vec_ref[0:1, :] + vec_ref[1:2, :]
+    n1_ref[...] = jnp.concatenate([normed, jnp.zeros((padded - rows, width), F32)], axis=0).astype(BF)
+    lse_ref[...] = jnp.zeros(lse_ref.shape, F32)
+    live = lax.broadcasted_iota(jnp.int32, (padded, 1), 0) < rows
+    for c, (ref, scale) in enumerate(((q_ref, HD ** (-0.5)), (k_ref, 1.0), (v_ref, 1.0))):
+        copies[c].wait()
+        for at in range(0, local, 256):
+            made = nn(n1_ref[...], w_buf[c, :, at : at + 256]) + bias_ref[c : c + 1, at : at + 256]
+            made = jnp.where(live, made, 0.0).astype(BF)
+            ref[:, at : at + 256] = made * jnp.asarray(scale, BF)
+    mask = key_mask(padded)
+    first = lane_halves()
+    lane = lax.broadcasted_iota(jnp.int32, (1, 128), 1)
+
+    def pair(p, carry):
+        cols = pl.ds(pl.multiple_of(p * 128, 128), 128)
+        keys, vals = k_ref[:, cols], v_ref[:, cols]
+        zero = jnp.zeros_like(keys)
+        own = (jnp.where(first, keys, zero), jnp.where(first, zero, keys))
+        for at, size in row_chunks(padded):
+            query = q_ref[at : at + size, cols]
+            outs = []
+            logs = lse_ref[at : at + size, :]
+            for h in range(2):
+                scores = times_back(query, own[h]) + mask
+                peak = jnp.max(scores, axis=-1, keepdims=True)
+                expo = jnp.exp(scores - peak)
+                total = jnp.sum(expo, axis=-1, keepdims=True)
+                probs = (expo * (1.0 / total)).astype(BF)
+                outs.append(nn(probs, vals))
+                logs = jnp.where(lane == 2 * p + h, peak + jnp.log(total), logs)
+            lse_ref[at : at + size, :] = logs
+            mixed_ref[at : at + size, cols] = jnp.where(first, outs[0], outs[1]).astype(BF)
+        return carry
+
+    lax.fori_loop(0, local // 128, pair, 0)
+    for at in range(0, width, 256):
+        made = nn(mixed_ref[...], wo_ref[:, at : at + 256])
+        part_ref[:, at : at + 256] = made[:rows].astype(BF)
+
+
+def attend(x, vec, bias, w3, w_out):
+    rows, width = x.shape
+    local = w3.shape[2]
+    padded = -(-rows // 16) * 16
+    wide = shape_of((padded, local), BF)
+    outs = (
+        shape_of((rows, width), BF),
+        wide,
+        wide,
+        wide,
+        wide,
+        shape_of((padded, width), BF),
+        shape_of((padded, 128), F32),
+    )
+    return call(
+        attend_kernel,
+        (x, vec, bias, w3, w_out),
+        [VM, VM, VM, ANY, VM],
+        outs,
+        (VM,) * 7,
+        [pltpu.VMEM((3, width, local), BF), pltpu.SemaphoreType.DMA((3,))],
+        name="attend",
+    )
+
+
+def grad_act_kernel(mask_ref, cot_ref, wd_ref, ga_ref, bd_ref, go):
+    @pl.when(pl.program_id(0) == 0)
+    def _():
+        masked = cot_ref[...].astype(F32) * mask_ref[0].astype(F32)
+        go[...] = masked.astype(BF)
+        bd_ref[...] = jnp.sum(masked, axis=0, keepdims=True)
+
+    ga_ref[...] = times_back(go[...], wd_ref[...]).astype(BF)
+
+
+def grad_act_of(mask, cot, w_down):
+    rows, width = cot.shape
+    hidden = w_down.shape[0]
+    tile = 512
+    return call(
+        grad_act_kernel,
+        (mask, cot, w_down),
+        [pl.BlockSpec((rows, width), lambda j, m: (0, 0)), pl.BlockSpec((tile, width), lambda j, m: (j, 0))],
+        (shape_of((rows, hidden), BF), shape_of((1, width), F32)),
+        (pl.BlockSpec((rows, tile), lambda j, m: (0, j)), pl.BlockSpec((1, width), lambda j, m: (0, 0))),
+        [pltpu.VMEM((rows, width), BF)],
+        (hidden // tile,),
+        name="grad_act",
+        prefetch=1,
+    )
+
+
+LANES = ((0, 20, 0), (20, 24, 1), (44, 20, 2))
+
+
+def feed_kernel(
+    mask_ref, sides_ref, x_ref, pa_ref, pb_ref, vec_ref, cot_ref, wu_ref, ub_ref, ga_ref,
+    act_ref, gp_ref, bu_ref, ka_ref, sa_ref, kb_ref, sb_ref, kc_ref, sc_ref, n2, go, grads, sems,
+):
+    step = pl.program_id(0)
+    steps = pl.num_programs(0)
+    tile = wu_ref.shape[1]
+    width = x_ref.shape[1]
+    blocks = tile // 64
+
+    @pl.when(step == 0)
+    def _():
+        resid = x_ref[...].astype(F32) + (pa_ref[...].astype(F32) + pb_ref[...].astype(F32)) + vec_ref[2:3, :]
+        unit, _ = normal_unit(resid)
+        n2[...] = (unit * vec_ref[3:4, :] + vec_ref[4:5, :]).astype(BF)
+        go[...] = (cot_ref[...].astype(F32) * mask_ref[0].astype(F32)).astype(BF)
+
+    pre = nn(n2[...], wu_ref[...]) + ub_ref[...].astype(F32)
+    cdf = 0.5 * (1.0 + lax.erf(pre * (0.5**0.5)))
+    act = (pre * cdf).astype(BF)
+    slope = cdf + pre * jnp.exp(-0.5 * pre * pre) * ((0.5 / jnp.pi) ** 0.5)
+    grad_pre = (ga_ref[...].astype(F32) * slope).astype(BF)
+    act_ref[...] = act
+    gp_ref[...] = grad_pre
+    bu_ref[...] = jnp.sum(grad_pre.astype(F32), axis=0, keepdims=True)
+    down = inner_rows(act, go[...]).astype(BF)
+    grads[pl.ds(step * blocks, blocks)] = down.reshape(blocks, 2, 32, width)
+    up = inner_rows(n2[...], grad_pre).astype(BF)
+    per = width // tile
+    cols = pl.ds(pl.multiple_of(lax.rem(step, per) * tile, tile), tile)
+    grads[pl.ds(steps * blocks, width // 32), step // per, :, cols] = up.reshape(width // 32, 32, tile)
+
+    def pieces(lane, keep, send):
+        first, count, bit = LANES[lane]
+        half, side = count // 2, sides_ref[bit]
+        return (
+            pltpu.make_async_copy(grads.at[pl.ds(first + side * half, half)], keep, sems.at[2 * lane]),
+            pltpu.make_async_copy(grads.at[pl.ds(first + (1 - side) * half, half)], send, sems.at[2 * lane + 1]),
+        )
+
+    early = pieces(0, ka_ref, sa_ref)
+
+    @pl.when(step == LANES[0][1] // blocks)
+    def _():
+        for copy in early:
+            copy.start()
+
+    @pl.when(step == steps - 1)
+    def _():
+        late = pieces(2, kc_ref, sc_ref) + pieces(1, kb_ref, sb_ref)
+        for copy in late:
+            copy.start()
+        for copy in early + late:
+            copy.wait()
+
+
+def feed(mask, sides, x, pa, pb, vec, cot, w_up, up_bias, ga):
+    rows, width = x.shape
+    hidden = w_up.shape[1]
+    tile = 256
+    fixed = pl.BlockSpec((rows, width), lambda j, m, s: (0, 0))
+    cols = pl.BlockSpec((rows, tile), lambda j, m, s: (0, j))
+    bias = pl.BlockSpec((1, tile), lambda j, m, s: (0, j))
+    lanes = []
+    for _, count, _ in LANES:
+        lanes += [shape_of((count // 2, 2, 32, width), BF)] * 2
+    return call(
+        feed_kernel,
+        (mask, sides, x, pa, pb, vec, cot, w_up, up_bias, ga),
+        [
+            fixed,
+            fixed,
+            fixed,
+            pl.BlockSpec((8, width), lambda j, m, s: (0, 0)),
+            fixed,
+            pl.BlockSpec((width, tile), lambda j, m, s: (0, j)),
+            bias,
+            cols,
+        ],
+        (shape_of((rows, hidden), BF), shape_of((rows, hidden), BF), shape_of((1, hidden), F32), *lanes),
+        (cols, cols, bias) + (ANY,) * 6,
+        [
+            pltpu.VMEM((rows, width), BF),
+            pltpu.VMEM((rows, width), BF),
+            pltpu.VMEM((2 * hidden // 64, 2, 32, width), BF),
+            pltpu.SemaphoreType.DMA((6,)),
+        ],
+        (hidden // tile,),
+        name="feed",
+        prefetch=2,
+    )
+
+
+def back_up_kernel(gp_ref, wu_ref, out_ref):
+    out_ref[...] = times_back(gp_ref[...], wu_ref[...]).astype(BF)
+
+
+def back_up(gp, w_up):
+    rows, hidden = gp.shape
+    width = w_up.shape[0]
+    return call(
+        back_up_kernel,
+        (gp, w_up),
+        [pl.BlockSpec((rows, hidden), lambda j: (0, 0)), pl.BlockSpec((256, hidden), lambda j: (j, 0))],
+        shape_of((rows, width), BF),
+        pl.BlockSpec((rows, 256), lambda j: (0, j)),
+        grid=(width // 256,),
+        name="back_up",
+    )
+
+
+def down_kernel(act_ref, wd_ref, out_ref):
+    out_ref[...] = nn(act_ref[...], wd_ref[...]).astype(BF)
+
+
+def down(act, w_down):
+    rows, hidden = act.shape
+    width = w_down.shape[1]
+    return call(
+        down_kernel,
+        (act, w_down),
+        [pl.BlockSpec((rows, hidden), lambda j: (0, 0)), pl.BlockSpec((hidden, 256), lambda j: (0, j))],
+        shape_of((rows, width), BF),
+        pl.BlockSpec((rows, 256), lambda j: (0, j)),
+        grid=(width // 256,),
+        name="down",
+    )
+
+
+def resid_back_kernel(
+    mask_ref, sides_ref, x_ref, pa_ref, pb_ref, vec_ref, ga_ref, gb_ref, cot_ref, mixed_ref, wo_ref,
+    gr_ref, gm_ref, sums_ref, keep_ref, send_ref, low, grads, sems,
+):
+    rows, width = x_ref.shape
+    padded, local = mixed_ref.shape
+    resid = x_ref[...].astype(F32) + (pa_ref[...].astype(F32) + pb_ref[...].astype(F32)) + vec_ref[2:3, :]
+    unit, inv = normal_unit(resid)
+    grad = ga_ref[...].astype(F32) + gb_ref[...].astype(F32)
+    total = cot_ref[...].astype(F32) * mask_ref[0].astype(F32) + norm_back(unit, inv, vec_ref[3:4, :], grad)
+    gr_ref[...] = total
+    low[...] = jnp.concatenate([total, jnp.zeros((padded - rows, width), F32)], axis=0).astype(BF)
+    sums_ref[...] = jnp.concatenate(
+        [
+            jnp.sum(total, axis=0, keepdims=True),
+            jnp.sum(grad * unit, axis=0, keepdims=True),
+            jnp.sum(grad, axis=0, keepdims=True),
+            jnp.zeros((5, width), F32),
+        ],
+        axis=0,
+    )
+    for at in range(0, width, 256):
+        grads[:, at : at + 256] = inner_rows(mixed_ref[...], low[:, at : at + 256]).astype(BF)
+    half, side = local // 2, sides_ref[1]
+    copies = (
+        pltpu.make_async_copy(grads.at[pl.ds(pl.multiple_of(side * half, half), half)], keep_ref, sems.at[0]),
+        pltpu.make_async_copy(grads.at[pl.ds(pl.multiple_of((1 - side) * half, half), half)], send_ref, sems.at[1]),
+    )
+    for copy in copies:
+        copy.start()
+    for at in range(0, local, 256):
+        gm_ref[:, at : at + 256] = times_back(low[...], wo_ref[at : at + 256, :]).astype(BF)
+    for copy in copies:
+        copy.wait()
+
+
+def resid_back(mask, sides, x, pa, pb, vec, ga, gb, cot, mixed, w_out):
+    rows, width = x.shape
+    padded, local = mixed.shape
+    return call(
+        resid_back_kernel,
+        (mask, sides, x, pa, pb, vec, ga, gb, cot, mixed, w_out),
+        [VM] * 9,
+        (
+            shape_of((rows, width), F32),
+            shape_of((padded, local), BF),
+            shape_of((8, width), F32),
+            shape_of((local // 2, width), BF),
+            shape_of((local // 2, width), BF),
+        ),
+        (VM, VM, VM, ANY, ANY),
+        [pltpu.VMEM((padded, width), BF), pltpu.VMEM((local, width), BF), pltpu.SemaphoreType.DMA((2,))],
+        name="resid_back",
+        prefetch=2,
+    )
+
+
+def attend_back_kernel(q_ref, k_ref, v_ref, mixed_ref, gm_ref, lse_ref, out_ref, probs_s, slopes_s):
+    padded, local = q_ref.shape
+    mask = key_mask(padded)
+    first = lane_halves()
+    lane = lax.broadcasted_iota(jnp.int32, (1, 128), 1)
+
+    def pair(p, carry):
+        cols = pl.ds(pl.multiple_of(p * 128, 128), 128)
+        keys, vals = k_ref[:, cols], v_ref[:, cols]
+        zero = jnp.zeros_like(keys)
+        own_k = (jnp.where(first, keys, zero), jnp.where(first, zero, keys))
+        own_v = (jnp.where(first, vals, zero), jnp.where(first, zero, vals))
+        for at, size in row_chunks(padded):
+            query = q_ref[at : at + size, cols]
+            grad = gm_ref[at : at + size, cols]
+            both = grad.astype(F32) * mixed_ref[at : at + size, cols].astype(F32)
+            logs = lse_ref[at : at + size, :]
+            outs = []
+            for h in range(2):
+                own_lanes = first if h == 0 else jnp.logical_not(first)
+                delta = jnp.sum(jnp.where(own_lanes, both, 0.0), axis=-1, keepdims=True)
+                log = jnp.sum(jnp.where(lane == 2 * p + h, logs, 0.0), axis=-1, keepdims=True)
+                probs = jnp.exp(times_back(query, own_k[h]) + mask - log)
+                slope = (probs * (times_back(grad, own_v[h]) - delta)).astype(BF)
+                probs_s[h, at : at + size, :] = probs.astype(BF)
+                slopes_s[h, at : at + size, :] = slope
+                outs.append(nn(slope, keys))
+            out_ref[at : at + size, cols] = (jnp.where(first, outs[0], outs[1]) * HD ** (-0.5)).astype(BF)
+        grad_t = gm_ref[:, cols].astype(F32).T.astype(BF)
+        query_t = q_ref[:, cols].astype(F32).T.astype(BF)
+        grad_k = [nn(query_t[HD * h : HD * h + HD], slopes_s[h]) for h in range(2)]
+        grad_v = [nn(grad_t[HD * h : HD * h + HD], probs_s[h]) for h in range(2)]
+        cols_k = pl.ds(pl.multiple_of(local + p * 128, 128), 128)
+        cols_v = pl.ds(pl.multiple_of(2 * local + p * 128, 128), 128)
+        out_ref[:, cols_k] = jnp.concatenate(grad_k, axis=0).T.astype(BF)
+        out_ref[:, cols_v] = jnp.concatenate(grad_v, axis=0).T.astype(BF)
+        return carry
+
+    lax.fori_loop(0, local // 128, pair, 0)
+
+
+def attend_back(q, k, v, mixed, gm, lse):
+    padded, local = q.shape
+    return call(
+        attend_back_kernel,
+        (q, k, v, mixed, gm, lse),
+        [VM] * 6,
+        shape_of((padded, 3 * local), BF),
+        VM,
+        [pltpu.VMEM((2, padded, padded), BF), pltpu.VMEM((2, padded, padded), BF)],
+        name="attend_back",
+    )
+
+
+def qkv_grad_kernel(sides_ref, n1_ref, g_ref, bias_ref, ka_ref, sa_ref, kb_ref, sb_ref, grads, sems):
+    width = n1_ref.shape[1]
+    local = g_ref.shape[1] // 3
+    for at in range(0, width, 256):
+        made = inner_rows(n1_ref[:, at : at + 256], g_ref[...]).astype(BF)
+        for c in range(3):
+            grads[c * width + at : c * width + at + 256, :] = made[:, c * local : (c + 1) * local]
+    half = 3 * width // 4
+    sx, sz = sides_ref[0], sides_ref[2]
+    copies = [
+        pltpu.make_async_copy(grads.at[pl.ds(pl.multiple_of(start, 256), half)], ref, sems.at[i])
+        for i, (start, ref) in enumerate(
+            (
+                (sx * half, ka_ref),
+                ((1 - sx) * half, sa_ref),
+                ((2 + sz) * half, kb_ref),
+                ((3 - sz) * half, sb_ref),
+            )
+        )
+    ]
+    for copy in copies:
+        copy.start()
+    bias_ref[...] = jnp.sum(g_ref[...].astype(F32), axis=0, keepdims=True)
+    for copy in copies:
+        copy.wait()
+
+
+def qkv_grad(sides, n1, grads):
+    width = n1.shape[1]
+    local = grads.shape[1] // 3
+    part = shape_of((3 * width // 4, local), BF)
+    return call(
+        qkv_grad_kernel,
+        (sides, n1, grads),
+        [VM, VM],
+        (shape_of((1, 3 * local), F32), part, part, part, part),
+        (VM, ANY, ANY, ANY, ANY),
+        [pltpu.VMEM((3 * width, local), BF), pltpu.SemaphoreType.DMA((4,))],
+        name="qkv_grad",
+        prefetch=1,
+    )
+
+
+def back_in_kernel(g_ref, w_ref, out_ref):
+    rows = out_ref.shape[0]
+    local = w_ref.shape[2]
+    total = times_back(g_ref[:, :local], w_ref[0])
+    for c in range(1, 3):
+        total += times_back(g_ref[:, c * local : (c + 1) * local], w_ref[c])
+    out_ref[...] = total[:rows].astype(BF)
+
+
+def back_in(grads, w3, rows):
+    padded = grads.shape[0]
+    _, width, local = w3.shape
+    return call(
+        back_in_kernel,
+        (grads, w3),
+        [
+            pl.BlockSpec((padded, 3 * local), lambda j: (0, 0)),
+            pl.BlockSpec((3, 256, local), lambda j: (0, j, 0)),
+        ],
+        shape_of((rows, width), BF),
+        pl.BlockSpec((rows, 256), lambda j: (0, j)),
+        grid=(width // 256,),
+        name="back_in",
+    )
+
+
+def images_back_kernel(x_ref, vec_ref, gr_ref, ga_ref, gb_ref, bd_ref, bu_ref, s2_ref, bq_ref, out_ref, pack_ref):
+    unit, inv = normal_unit(x_ref[...].astype(F32))
+    grad = ga_ref[...].astype(F32) + gb_ref[...].astype(F32)
+    out_ref[...] = (gr_ref[...] + norm_back(unit, inv, vec_ref[0:1, :], grad)).astype(BF)
+    width = x_ref.shape[1]
+    hidden = bu_ref.shape[1]
+    local = bq_ref.shape[1] // 3
+    pack_ref[0:1, :] = jnp.sum(grad * unit, axis=0, keepdims=True)
+    pack_ref[1:2, :] = jnp.sum(grad, axis=0, keepdims=True)
+    pack_ref[2:5, :] = s2_ref[0:3, :]
+    pack_ref[5:6, :] = bd_ref[...]
+    for i in range(hidden // width):
+        pack_ref[6 + i : 7 + i, :] = bu_ref[:, i * width : (i + 1) * width]
+    after = 6 + hidden // width
+    pack_ref[after : after + 1, :local] = bq_ref[:, :local]
+    pack_ref[after : after + 1, local:] = bq_ref[:, 2 * local :]
+    pack_ref[after + 1 :, :] = jnp.zeros((pack_ref.shape[0] - after - 1, width), F32)
+
+
+def images_back(x, vec, gr, ga, gb, bd, bu, s2, bq):
+    return call(
+        images_back_kernel,
+        (x, vec, gr, ga, gb, bd, bu, s2, bq),
+        [VM] * 9,
+        (shape_of(x.shape, BF), shape_of((16, x.shape[1]), F32)),
+        (VM, VM),
+        name="images_back",
+    )
+
+
+def block_out_kernel(x_ref, pa_ref, pb_ref, vec_ref, ma_ref, mb_ref, out_ref):
+    resid = x_ref[...].astype(F32) + (pa_ref[...].astype(F32) + pb_ref[...].astype(F32)) + vec_ref[2:3, :]
+    out_ref[...] = (resid + (ma_ref[...].astype(F32) + mb_ref[...].astype(F32)) + vec_ref[5:6, :]).astype(BF)
+
+
+def block_out(x, pa, pb, vec, ma, mb):
+    return call(block_out_kernel, (x, pa, pb, vec, ma, mb), [VM] * 6, shape_of(x.shape, BF), VM, name="block_out")
+
+
+def add_split_kernel(sides_ref, k0_ref, k1_ref, r0_ref, r1_ref, keep_ref, send_ref):
+    keep_ref[...] = (k0_ref[...].astype(F32) + r0_ref[...].astype(F32)).astype(BF)
+    send_ref[...] = (k1_ref[...].astype(F32) + r1_ref[...].astype(F32)).astype(BF)
+
+
+def add_split(sides, bit, keep, recv):
+    rows, width = keep.shape
+    half = rows // 2
+    count = 2 if half % 32 == 0 and half >= 256 else 1
+    block = (half // count, width)
+    own = pl.BlockSpec(block, lambda i, s: (s[bit] * count + i, 0))
+    other = pl.BlockSpec(block, lambda i, s: ((1 - s[bit]) * count + i, 0))
+    out = pl.BlockSpec(block, lambda i, s: (i, 0))
+    return call(
+        add_split_kernel,
+        (sides, keep, keep, recv, recv),
+        [own, other, own, other],
+        (shape_of((half, width), BF),) * 2,
+        (out, out),
+        grid=(count,),
+        name="add_split",
+        prefetch=1,
+        vmem=16,
+    )
+
+
+def add_kernel(a_ref, b_ref, out_ref):
+    out_ref[...] = (a_ref[...].astype(F32) + b_ref[...].astype(F32)).astype(out_ref.dtype)
+
+
+def add(a, b):
+    return call(add_kernel, (a, b), [VM, VM], shape_of(a.shape, a.dtype), VM, name="add", vmem=16)
+
+
+def join_kernel(sides_ref, own_ref, other_ref, out_ref, sems, *, bit):
+    half = own_ref.shape[0]
+    side = sides_ref[bit]
+    copies = (
+        pltpu.make_async_copy(own_ref, out_ref.at[pl.ds(pl.multiple_of(side * half, 16), half)], sems.at[0]),
+        pltpu.make_async_copy(other_ref, out_ref.at[pl.ds(pl.multiple_of((1 - side) * half, 16), half)], sems.at[1]),
+    )
+    for copy in copies:
+        copy.start()
+    for copy in copies:
+        copy.wait()
+
+
+def join(sides, bit, own, other):
+    half, width = own.shape
+
+    def body(*refs):
+        join_kernel(*refs, bit=bit)
+
+    return call(
+        body,
+        (sides, own, other),
+        [ANY, ANY],
+        shape_of((2 * half, width), BF),
+        ANY,
+        [pltpu.SemaphoreType.DMA((2,))],
+        name="join",
+        prefetch=1,
+        vmem=8,
+    )
+
+
+def finish_kernel(sides_ref, own_ref, other_ref, *rest):
+    out_ref = rest[-1]
+
+    @pl.when(pl.program_id(0) == 0)
+    def _():
+        out_ref[...] = own_ref[...].astype(F32).reshape(out_ref.shape)
+
+    @pl.when(pl.program_id(0) == 1)
+    def _():
+        out_ref[...] = other_ref[...].astype(F32).reshape(out_ref.shape)
+
+
+def finish(sides, bit, own, other, target, shape, start, block):
+    half, width = own.shape
+    count = half // block
+    base = start // block
+    spec_own = pl.BlockSpec((block, width), lambda t, i, s: (jnp.where(t == 0, i, count - 1), 0))
+    spec_other = pl.BlockSpec((block, width), lambda t, i, s: (jnp.where(t == 0, 0, i), 0))
+    out = pl.BlockSpec(
+        (block, width), lambda t, i, s: (base + jnp.where(t == 0, s[bit], 1 - s[bit]) * count + i, 0)
+    )
+    args, specs, aliases = (sides, own, other), [spec_own, spec_other], {}
+    if target is not None:
+        args, specs, aliases = args + (target,), specs + [ANY], {3: 0}
+    return call(
+        finish_kernel, args, specs, shape_of(shape, F32), out, grid=(2, count), aliases=aliases, name="finish", prefetch=1
+    )
+
+
+def rows_pair(values):
+    rows, width = values.shape
+    split = values.reshape(rows // 64, 2, 32, width)
+    return jnp.concatenate([split[:, 0], split[:, 1]], axis=-1).reshape(rows // 2, 2 * width)
+
+
+def finish_up_kernel(sides_ref, own_ref, other_ref, *rest):
+    out_ref = rest[-1]
+
+    @pl.when(pl.program_id(0) == 0)
+    def _():
+        out_ref[...] = rows_pair(own_ref[...].astype(F32))
+
+    @pl.when(pl.program_id(0) == 1)
+    def _():
+        out_ref[...] = rows_pair(other_ref[...].astype(F32))
+
+
+def finish_up(sides, bit, own, other, shape, start, block):
+    half, width = own.shape
+    count = half // block
+    base = start // (block // 2)
+    spec_own = pl.BlockSpec((block, width), lambda t, i, s: (jnp.where(t == 0, i, count - 1), 0))
+    spec_other = pl.BlockSpec((block, width), lambda t, i, s: (jnp.where(t == 0, 0, i), 0))
+    out = pl.BlockSpec(
+        (block // 2, 2 * width), lambda t, i, s: (base + jnp.where(t == 0, s[bit], 1 - s[bit]) * count + i, 0)
+    )
+    return call(
+        finish_up_kernel,
+        (sides, own, other),
+        [spec_own, spec_other],
+        shape_of(shape, F32),
+        out,
+        grid=(2, count),
+        name="finish_up",
+        prefetch=1,
+    )
+
+
+def finish_both(sides, bit, own, other, down_target, up_target, start, block):
+    half, width = own.shape
+    count = half // block
+    base = start // block
+    spec = pl.BlockSpec((block, width), lambda i, s: (i, 0))
+
+    def body(sides_ref, own_ref, other_ref, d_in, u_in, d_ref, u_ref):
+        @pl.when(sides_ref[bit] == 0)
+        def _():
+            d_ref[...] = own_ref[...].astype(F32)
+            u_ref[...] = rows_pair(other_ref[...].astype(F32))
+
+        @pl.when(sides_ref[bit] == 1)
+        def _():
+            d_ref[...] = other_ref[...].astype(F32)
+            u_ref[...] = rows_pair(own_ref[...].astype(F32))
+
+    return call(
+        body,
+        (sides, own, other, down_target, up_target),
+        [spec, spec, ANY, ANY],
+        (shape_of(down_target.shape, F32), shape_of(up_target.shape, F32)),
+        (
+            pl.BlockSpec((block, width), lambda i, s: (base + i, 0)),
+            pl.BlockSpec((block // 2, 2 * width), lambda i, s: (i, 0)),
+        ),
+        grid=(count,),
+        aliases={3: 0, 4: 1},
+        name="finish_both",
+        prefetch=1,
+    )
+
+
+class Lane:
+    def __init__(self, sides, keep, send, order, swap):
+        self.sides, self.order, self.swap = sides, order, swap
+        self.keep, self.send = keep, send
+        self.stage = 0
+
+    def step(self):
+        stage, order = self.stage, self.order
+        self.stage += 1
+        if stage < 2:
+            recv = lax.ppermute(self.send, "dp", xor_pairs(1 << order[stage]))
+            self.keep, self.send = add_split(self.sides, order[stage + 1], self.keep, recv)
+        elif stage == 2:
+            self.keep = add(self.keep, lax.ppermute(self.send, "dp", xor_pairs(1 << order[2])))
+        elif stage == 3:
+            self.keep = add(self.keep, lax.ppermute(self.keep, "dp", xor_pairs(self.swap)))
+        elif stage < 6:
+            bit = order[6 - stage]
+            recv = lax.ppermute(self.keep, "dp", xor_pairs(1 << bit))
+            self.keep = join(self.sides, bit, self.keep, recv)
+        else:
+            self.send = lax.ppermute(self.keep, "dp", xor_pairs(1 << order[0]))
+
+
+def shards_cube(
+    images,
+    image_mask,
+    cotangent,
+    ln1_gain,
+    ln1_bias,
+    w_qkv,
+    qv_bias,
+    w_out,
+    out_bias,
+    ln2_gain,
+    ln2_bias,
+    w_up,
+    up_bias,
+    w_down,
+    down_bias,
+):
+    _, rows, width = images.shape
+    local = w_qkv.shape[2]
+    hidden = w_up.shape[1]
+    x = images.reshape(rows, width)
+    cot = cotangent.reshape(rows, width)
+    index = lax.axis_index("dp")
+    sides = jnp.stack([index & 1, (index >> 1) & 1, (index >> 2) & 1]).astype(jnp.int32)
+    zeros = jnp.zeros((width,), BF)
+    vec = jnp.stack(
+        [ln1_gain, ln1_bias, out_bias, ln2_gain, ln2_bias, down_bias, zeros, zeros]
+    ).astype(F32)
+    bias = jnp.stack([qv_bias[0], jnp.zeros_like(qv_bias[0]), qv_bias[1]]).astype(F32)
+    w3 = jnp.transpose(w_qkv, (1, 0, 2))
+    swap = [(0, 1), (1, 0)]
+
+    part, q, k, v, mixed, n1, lse = attend(x, vec, bias, w3, w_out)
+    part_b = lax.ppermute(part, "tensor", swap)
+    ga, bd = grad_act_of(image_mask, cot, w_down)
+    act, gp, bu, ka, sa, kb, sb, kc, sc = feed(
+        image_mask, sides, x, part, part_b, vec, cot, w_up, up_bias.reshape(1, hidden), ga
+    )
+    flat = [piece.reshape(-1, width) for piece in (ka, sa, kb, sb, kc, sc)]
+    lane_a = Lane(sides, flat[0], flat[1], (0, 1, 2), 8)
+    lane_b = Lane(sides, flat[2], flat[3], (1, 2, 0), 8)
+    lane_c = Lane(sides, flat[4], flat[5], (2, 0, 1), 8)
+    gn2 = back_up(gp, w_up)
+    gn2_b = lax.ppermute(gn2, "tensor", swap)
+    mlp = down(act, w_down)
+    mlp_b = lax.ppermute(mlp, "tensor", swap)
+    gr, gm, s2, ko, so = resid_back(image_mask, sides, x, part, part_b, vec, gn2, gn2_b, cot, mixed, w_out)
+    lane_o = Lane(sides, ko, so, (1, 2, 0), 8)
+    grads = attend_back(q, k, v, mixed, gm, lse)
+    bq, kqa, sqa, kqb, sqb = qkv_grad(sides, n1, grads)
+    lane_qa = Lane(sides, kqa, sqa, (0, 1, 2), 8)
+    lane_qb = Lane(sides, kqb, sqb, (2, 0, 1), 8)
+    gn1 = back_in(grads, w3, rows)
+    gn1_b = lax.ppermute(gn1, "tensor", swap)
+    images_grad, pack = images_back(x, vec, gr, gn1, gn1_b, bd, bu, s2, bq)
+    block_output = block_out(x, part, part_b, vec, mlp, mlp_b)
+
+    for _ in range(7):
+        for lane in (lane_a, lane_c, lane_b, lane_o, lane_qa, lane_qb):
+            lane.step()
+    for bit in (1, 2, 4, 8):
+        pack = add(pack, lax.ppermute(pack, "dp", xor_pairs(bit)))
+    g_down = finish(sides, 0, lane_a.keep, lane_a.send, None, (hidden, width), 0, 128)
+    g_up = finish_up(sides, 2, lane_c.keep, lane_c.send, (width, hidden), 384, 128)
+    g_down, g_up = finish_both(sides, 1, lane_b.keep, lane_b.send, g_down, g_up, 1280, 128)
+    g_out = finish(sides, 1, lane_o.keep, lane_o.send, None, (local, width), 0, 128)
+    g_qkv = finish(sides, 0, lane_qa.keep, lane_qa.send, None, (3 * width, local), 0, 256)
+    g_qkv = finish(sides, 2, lane_qb.keep, lane_qb.send, g_qkv, (3 * width, local), 3 * width // 2, 256)
+    g_qkv = jnp.transpose(g_qkv.reshape(3, width, local), (1, 0, 2))
+    after = 6 + hidden // width
+    return (
+        block_output.reshape(images.shape),
+        images_grad.reshape(images.shape),
+        pack[0],
+        pack[1],
+        g_qkv,
+        pack[after].reshape(2, local),
+        g_out,
+        pack[2],
+        pack[3],
+        pack[4],
+        g_up,
+        pack[6:after].reshape(hidden),
+        g_down,
+        pack[5],
+    )
+
+
+def shards(*args):
+    images, w_up = args[0], args[11]
+    cube = lax.axis_size("dp") == 16 and lax.axis_size("tensor") == 2
+    if cube and images.shape[0] == 1 and w_up.shape[1] == 2 * w_up.shape[0]:
+        return shards_cube(*args)
+    return shards_any(*args)
+
+
 def solution(mesh):
     in_specs = (
         P("dp", None, None),

time: 574 us -> 383 us (0.67)
  Pallas kernels: 0 us -> 143 us
  other arithmetic: 110 us -> 0.16 us
  matrix products: 109 us -> 0 us
  starting transfers between devices: 107 us -> 46.9 us
  local copies, waits for them, and re-layouts: 55.6 us -> 26.5 us
  waiting for transfers between devices: 185 us -> 163 us
    pallas_call x0 -> x57, Pallas kernels: none -> 143 us  [call(): pl.pallas_call(body, out_shape=outs, grid_spec=spec, input_output_aliases...]
    dot_general x18 -> x0, matrix products: 109 us -> none  [the longest x1 22.9 us: attend_backward(): jnp.einsum('hqk,khd->qhd', grad_scores, keyset, preferred_element_type=F32)]
    ppermute x92 -> x50, starting transfers between devices: 107 us -> 46.9 us  [the longest x12 16.4 us: step(): recv = lax.ppermute(self.send, 'dp', xor_pairs(1 << order[stage]))]
    select_n x42 -> x0, other arithmetic: 58.6 us -> none  [sum_over_dp(): jnp.where(side == 0, jnp.concatenate([piece, other], axis=0), jnp.concate...]
    ppermute x92 -> x50, waiting for transfers between devices: 185 us -> 163 us  [the longest x12 59.1 us: step(): recv = lax.ppermute(self.keep, 'dp', xor_pairs(1 << bit))]
    concatenate x13 -> x0, local copies, waits for them, and re-layouts: 18.8 us -> none  [the longest x12 18.8 us: sum_over_dp(): jnp.concatenate([piece, other], axis=0)]
    add x53 -> x0, other arithmetic: 18.2 us -> none  [the longest x36 11.9 us: sum_over_dp(): pieces[lane] = kept + lax.ppermute(sent, 'dp', xor_pairs(bit))]
    reduce_sum x9 -> x0, other arithmetic: 16.2 us -> none  [the longest x1 3.53 us: shards(): jnp.sum(grad_resid, axis=0)]
  transfers between devices with their start and end apart: 92 -> 50, of which waited for: 39 -> 18; matrix products, arithmetic and copies ran while one was open for 36% -> 1% of each run, Pallas kernels for 0% -> 25%
where the time goes in v2:
time: 383 us; the launch traced here: 382 us
  waiting for transfers between devices  163 us (43%)
  Pallas kernels  143 us (37%)
  starting transfers between devices  46.9 us (12%)
  local copies, waits for them, and re-layouts  26.5 us (7%)
    pallas_call x57, Pallas kernels, call(): pl.pallas_call(body, out_shape=outs, grid_spec=spec, input_output_aliases...  143 us
    ppermute x12, waiting for transfers between devices, step(): recv = lax.ppermute(self.keep, 'dp', xor_pairs(1 << bit))  59.1 us
    ppermute x12, waiting for transfers between devices, step(): recv = lax.ppermute(self.send, 'dp', xor_pairs(1 << order[stage]))  37.9 us
    ppermute x6, waiting for transfers between devices, step(): lax.ppermute(self.send, 'dp', xor_pairs(1 << order[2]))  23.5 us
    ppermute x6, waiting for transfers between devices, step(): lax.ppermute(self.keep, 'dp', xor_pairs(self.swap))  20.6 us
    unnamed x74, local copies, waits for them, and re-layouts  20.2 us
    ppermute x4, waiting for transfers between devices, shards_cube(): pack = add(pack, lax.ppermute(pack, 'dp', xor_pairs(bit)))  19.9 us
    ppermute x12, starting transfers between devices, step(): recv = lax.ppermute(self.send, 'dp', xor_pairs(1 << order[stage]))  16.4 us
  transfers between devices with their start and end apart: 50, of which 18 were waited for; matrix products, arithmetic and copies ran while one was open for 1% of the time, Pallas kernels for 25%

profile of v2, /device:TPU:0, one launch (start us, length us, event | category | flops | bytes accessed | tf_op | source)
XLA Modules:
  0.0 381.7 jit_solution(15408899151802133636)
XLA Ops:
  10.2 18.0 %attend.1 = (bf16[584,1024]{1,0:T(8,128)(2,1)S(1)}, bf16[592,512]{1,0:T(8,128)(2,1)S(1)}, bf16[592,512]{1,0:T(8,128)(2,1)S(1)}, bf16[592,512]{1,0:T(8,128)(2,1)S...) custom-call(bf16[584,1024]{1,0:T(8,128)(2,1)S(1)} %bitcast.29, ...), custom_call_target="tpu_custom_call" | custom-call | tf_op jit(solution)/shard_map/attend/pallas_call | solution.py:283
  37.2 3.8 grad_act.1
  42.4 22.6 %feed.1 = (bf16[584,2048]{1,0:T(8,128)(2,1)}, bf16[584,2048]{1,0:T(8,128)(2,1)}, f32[1,2048]{1,0:T(1,128)S(1)}, bf16[10,2,32,1024]{3,2,1,0:T(8,128)(2,1)S(1)}, b...) custom-call(s32[1]{0:T(128)S(6)} %copy.38.mask_ref, ...), custom_call_target="tpu_custom_call" | custom-call | tf_op jit(solution)/shard_map/feed/pallas_call | solution.py:283
  78.0 3.9 %down.1.ma_ref = bf16[584,1024]{1,0:T(8,128)(2,1)S(1)} custom-call(bf16[584,2048]{1,0:T(8,128)(2,1)S(1)} %copy-done.20, bf16[2048,1024]{1,0:T(8,128)(2,1)S(1)} %copy-done.4), custom_call_target="tpu_custom_call" | custom-call | tf_op jit(solution)/shard_map/down/pallas_call | solution.py:283
  82.1 22.8 %collective-permute-done.29.r0_ref.r1_ref = bf16[768,1024]{1,0:T(8,128)(2,1)S(1)} collective-permute-done((bf16[768,1024]{1,0:T(8,128)(2,1)}, bf16[768,1024]{1,0:T(8,128)(2,1)S(1)}, u32[]{:S(2)}, u32[]{:S(2)}) %collective-permute-start.29) | collective-permute-done | bytes 1572896 | tf_op jit(solution)/shard_map/ppermute | solution.py:938
  108.4 5.0 %resid_back.1 = (f32[584,1024]{1,0:T(8,128)S(1)}, bf16[592,512]{1,0:T(8,128)(2,1)S(1)}, f32[8,1024]{1,0:T(8,128)S(1)}, bf16[256,1024]{1,0:T(8,128)(2,1)S(1)}, bf16[256,1024]{1,0:T(8,128)(2,1)}) custom-call(s32[1]{0:T(128)S(6)} %copy.38.mask_ref, s32[3]{0:T(128)S(1)} %pad_add_fusion.sides_ref.refs_0_, bf16[584,1024]{1,0:T(8,128)(2,1)S(1)} %bitcast.31, ...), custom_call_target="tpu_custom_call" | custom-call | tf_op jit(solution)/shard_map/resid_back/pallas_call | solution.py:283
  121.3 11.2 %attend_back.1.g_ref = bf16[592,1536]{1,0:T(8,128)(2,1)S(1)} custom-call(bf16[592,512]{1,0:T(8,128)(2,1)S(1)} %copy-done.27, bf16[592,512]{1,0:T(8,128)(2,1)S(1)} %copy-done.29, bf16[592,512]{1,0:T(8,128)(2,1)S(1)} %copy-done.31, bf16[592,512]{1,0:T(8,128)(2,1)S(1)} %copy-done.16, bf16[592,512]{1,0:T(8,128)(2,1)S(1)} %get-tuple-element.79.gm_ref, ...), custom_call_target="tpu_custom_call" | custom-call | tf_op jit(solution)/shard_map/attend_back/pallas_call | solution.py:283
  132.5 4.3 %qkv_grad.1 = (f32[1,1536]{1,0:T(1,128)S(1)}, bf16[768,512]{1,0:T(8,128)(2,1)S(1)}, bf16[768,512]{1,0:T(8,128)(2,1)S(1)}, bf16[768,512]{1,0:T(8,128)(2,1)S(1)}, bf16[768,512]{1,0:T(8,128)(2,1)}) custom-call(s32[3]{0:T(128)S(1)} %pad_add_fusion.sides_ref.refs_0_, bf16[592,1024]{1,0:T(8,128)(2,1)S(1)} %copy-done.25, bf16[592,1536]{1,0:T(8,128)(2,1)S(1)} %attend_back.1.g_ref), custom_call_target="tpu_custom_call" | custom-call | tf_op jit(solution)/shard_map/qkv_grad/pallas_call | solution.py:283
  141.0 9.3 %collective-permute-done.31.b_ref = bf16[192,1024]{1,0:T(8,128)(2,1)S(1)} collective-permute-done((bf16[192,1024]{1,0:T(8,128)(2,1)S(1)}, bf16[192,1024]{1,0:T(8,128)(2,1)S(1)}, u32[]{:S(2)}, u32[]{:S(2)}) %collective-permute-start.31) | collective-permute-done | bytes 393248 | tf_op jit(solution)/shard_map/ppermute | solution.py:941
  158.3 10.9 %collective-permute-done.23.r0_ref.r1_ref = bf16[128,1024]{1,0:T(8,128)(2,1)S(1)} collective-permute-done((bf16[128,1024]{1,0:T(8,128)(2,1)S(1)}, bf16[128,1024]{1,0:T(8,128)(2,1)S(1)}, u32[]{:S(2)}, u32[]{:S(2)}) %collective-permute-start.23) | collective-permute-done | bytes 262176 | tf_op jit(solution)/shard_map/ppermute | solution.py:938
  180.9 11.3 %collective-permute-done.24.b_ref = bf16[64,1024]{1,0:T(8,128)(2,1)S(1)} collective-permute-done((bf16[64,1024]{1,0:T(8,128)(2,1)S(1)}, bf16[64,1024]{1,0:T(8,128)(2,1)S(1)}, u32[]{:S(2)}, u32[]{:S(2)}) %collective-permute-start.24) | collective-permute-done | bytes 131104 | tf_op jit(solution)/shard_map/ppermute | solution.py:941
  192.2 3.6 collective-permute-start.46
  196.5 16.2 %collective-permute-done.25.b_ref = bf16[64,1024]{1,0:T(8,128)(2,1)S(1)} collective-permute-done((bf16[64,1024]{1,0:T(8,128)(2,1)S(1)}, bf16[64,1024]{1,0:T(8,128)(2,1)S(1)}, u32[]{:S(2)}, u32[]{:S(2)}) %collective-permute-start.25) | collective-permute-done | bytes 131104 | tf_op jit(solution)/shard_map/ppermute | solution.py:943
  224.8 4.2 %collective-permute-done.16.r0_ref.r1_ref = bf16[384,512]{1,0:T(8,128)(2,1)S(1)} collective-permute-done((bf16[384,512]{1,0:T(8,128)(2,1)S(1)}, bf16[384,512]{1,0:T(8,128)(2,1)S(1)}, u32[]{:S(2)}, u32[]{:S(2)}) %collective-permute-start.16) | collective-permute-done | bytes 393248 | tf_op jit(solution)/shard_map/ppermute | solution.py:938
  229.5 17.3 %collective-permute-done.40.refs_2_ = bf16[160,1024]{1,0:T(8,128)(2,1)S(1)} collective-permute-done((bf16[160,1024]{1,0:T(8,128)(2,1)S(1)}, bf16[160,1024]{1,0:T(8,128)(2,1)S(1)}, u32[]{:S(2)}, u32[]{:S(2)}) %collective-permute-start.40) | collective-permute-done | bytes 327712 | tf_op jit(solution)/shard_map/ppermute | solution.py:946
  255.3 12.1 %collective-permute-done.5.b_ref = f32[16,1024]{1,0:T(8,128)S(1)} collective-permute-done((f32[16,1024]{1,0:T(8,128)S(1)}, f32[16,1024]{1,0:T(8,128)S(1)}, u32[]{:S(2)}, u32[]{:S(2)}) %collective-permute-start.5) | collective-permute-done | bytes 65568 | tf_op jit(solution)/shard_map/ppermute | solution.py:1013
  269.0 4.0 %collective-permute-done.12.refs_2_ = bf16[192,512]{1,0:T(8,128)(2,1)S(1)} collective-permute-done((bf16[192,512]{1,0:T(8,128)(2,1)S(1)}, bf16[192,512]{1,0:T(8,128)(2,1)S(1)}, u32[]{:S(2)}, u32[]{:S(2)}) %collective-permute-start.12) | collective-permute-done | bytes 196640 | tf_op jit(solution)/shard_map/ppermute | solution.py:946
  276.4 4.4 %collective-permute-done.18.b_ref = bf16[192,512]{1,0:T(8,128)(2,1)S(1)} collective-permute-done((bf16[192,512]{1,0:T(8,128)(2,1)S(1)}, bf16[192,512]{1,0:T(8,128)(2,1)S(1)}, u32[]{:S(2)}, u32[]{:S(2)}) %collective-permute-start.18) | collective-permute-done | bytes 196640 | tf_op jit(solution)/shard_map/ppermute | solution.py:943
  293.5 37.7 %collective-permute-done.20.refs_2_ = bf16[384,512]{1,0:T(8,128)(2,1)S(1)} collective-permute-done((bf16[384,512]{1,0:T(8,128)(2,1)S(1)}, bf16[384,512]{1,0:T(8,128)(2,1)S(1)}, u32[]{:S(2)}, u32[]{:S(2)}) %collective-permute-start.20) | collective-permute-done | bytes 393248 | tf_op jit(solution)/shard_map/ppermute | solution.py:946
  348.9 5.5 %finish.4.rest_0_ = f32[3072,512]{1,0:T(8,128)} custom-call(s32[3]{0:T(128)S(1)} %pad_add_fusion.sides_ref.refs_0_, bf16[768,512]{1,0:T(8,128)(2,1)} %join.15.own_ref, bf16[768,512]{1,0:T(8,128)(2,1)} %collective-permute-done.21.other_ref), custom_call_target="tpu_custom_call" | custom-call | tf_op jit(solution)/shard_map/finish/pallas_call | solution.py:283
  354.4 5.0 %finish.5 = f32[3072,512]{1,0:T(8,128)} custom-call(s32[3]{0:T(128)S(1)} %pad_add_fusion.sides_ref.refs_0_, bf16[768,512]{1,0:T(8,128)(2,1)S(1)} %join.13.own_ref, bf16[768,512]{1,0:T(8,128)(2,1)} %collective-permute-done.14.other_ref, f32[3072,512]{1,0:T(8,128)} %finish.4.rest_0_), custom_call_target="tpu_custom_call", output_to_operand_aliasing={{}: (3, {})} | custom-call | tf_op jit(solution)/shard_map/finish/pallas_call | solution.py:283
  359.4 8.0 %finish_up.1.u_in = f32[1024,2048]{1,0:T(8,128)} custom-call(s32[3]{0:T(128)S(1)} %pad_add_fusion.sides_ref.refs_0_, bf16[640,1024]{1,0:T(8,128)(2,1)} %join.23.own_ref, bf16[640,1024]{1,0:T(8,128)(2,1)} %collective-permute-done.49.other_ref), custom_call_target="tpu_custom_call" | custom-call | tf_op jit(solution)/shard_map/finish_up/pallas_call | solution.py:283
  367.4 8.0 %finish.7.d_in = f32[2048,1024]{1,0:T(8,128)} custom-call(s32[3]{0:T(128)S(1)} %pad_add_fusion.sides_ref.refs_0_, bf16[640,1024]{1,0:T(8,128)(2,1)} %join.21.own_ref, bf16[640,1024]{1,0:T(8,128)(2,1)} %collective-permute-done.42.other_ref), custom_call_target="tpu_custom_call" | custom-call | tf_op jit(solution)/shard_map/finish/pallas_call | solution.py:283
  375.4 6.3 %finish_both.1 = (f32[2048,1024]{1,0:T(8,128)}, f32[1024,2048]{1,0:T(8,128)}) custom-call(s32[3]{0:T(128)S(1)} %pad_add_fusion.sides_ref.refs_0_, bf16[768,1024]{1,0:T(8,128)(2,1)} %join.19.own_ref, bf16[768,1024]{1,0:T(8,128)(2,1)} %collective-permute-done.35.other_ref, f32[2048,1024]{1,0:T(8,128)} %finish.7.d_in, ...), custom_call_target="tpu_custom_call", output_to_operand_aliasing={{0}: (3, {}), {1}: (4, {})} | custom-call | tf_op jit(solution)/shard_map/finish_both/pallas_call | solution.py:283
  (223 shorter events, 124.5 us)
Async XLA Ops:
  67.2 37.8 %collective-permute-start.29 = (bf16[768,1024]{1,0:T(8,128)(2,1)}, bf16[768,1024]{1,0:T(8,128)(2,1)S(1)}, u32[]{:S(2)}, u32[]{:S(2)}) collective-permute-start(bf16[768,1024]{1,0:T(8,128)(2,1)} %bitcast.16), channel_id=1, source_target_pairs={{0,4},{2,6},{4,0},{6,2},{8,12},{10,14},{12,8},{14,10},{16,20},{18,... | collective-permute-start | bytes 4718600 | tf_op jit(solution)/shard_map/ppermute | solution.py:938
  69.7 45.4 %collective-permute-start.36 = (bf16[640,1024]{1,0:T(8,128)(2,1)}, bf16[640,1024]{1,0:T(8,128)(2,1)}, u32[]{:S(2)}, u32[]{:S(2)}) collective-permute-start(bf16[640,1024]{1,0:T(8,128)(2,1)} %bitcast.18), channel_id=1, source_target_pairs={{0,2},{2,0},{4,6},{6,4},{8,10},{10,8},{12,14},{14,12},{16,18},{18,... | collective-permute-start | bytes 3932168 | tf_op jit(solution)/shard_map/ppermute | solution.py:938
  76.3 32.1 %collective-permute-start.2 = (bf16[584,1024]{1,0:T(8,128)(2,1)S(1)}, bf16[584,1024]{1,0:T(8,128)(2,1)S(1)}, u32[]{:S(2)}, u32[]{:S(2)}) collective-permute-start(bf16[584,1024]{1,0:T(8,128)(2,1)S(1)} %back_up.1.ga_ref), channel_id=1, source_target_pairs={{0,1},{1,0},{2,3},{3,2},{4,5},{5,4},{6,7},{7,6},{8,9},{9,8},{10,11... | collective-permute-start | bytes 3588104 | tf_op jit(solution)/shard_map/ppermute | solution.py:995
  76.4 41.8 %collective-permute-start.43 = (bf16[640,1024]{1,0:T(8,128)(2,1)}, bf16[640,1024]{1,0:T(8,128)(2,1)S(1)}, u32[]{:S(2)}, u32[]{:S(2)}) collective-permute-start(bf16[640,1024]{1,0:T(8,128)(2,1)} %bitcast.45), channel_id=1, source_target_pairs={{0,8},{2,10},{4,12},{6,14},{8,0},{10,2},{12,4},{14,6},{16,24},{18,... | collective-permute-start | bytes 3932168 | tf_op jit(solution)/shard_map/ppermute | solution.py:938
  81.9 56.3 %collective-permute-start.1 = (bf16[584,1024]{1,0:T(8,128)(2,1)S(1)}, bf16[584,1024]{1,0:T(8,128)(2,1)}, u32[]{:S(2)}, u32[]{:S(2)}) collective-permute-start(bf16[584,1024]{1,0:T(8,128)(2,1)S(1)} %down.1.ma_ref), channel_id=1, source_target_pairs={{0,1},{1,0},{2,3},{3,2},{4,5},{5,4},{6,7},{7,6},{8,9},{9,8},{10,11... | collective-permute-start | bytes 3588104 | tf_op jit(solution)/shard_map/ppermute | solution.py:997
  106.6 30.1 %collective-permute-start.30 = (bf16[384,1024]{1,0:T(8,128)(2,1)}, bf16[384,1024]{1,0:T(8,128)(2,1)S(1)}, u32[]{:S(2)}, u32[]{:S(2)}) collective-permute-start(bf16[384,1024]{1,0:T(8,128)(2,1)} %get-tuple-element.109), channel_id=1, source_target_pairs={{0,8},{2,10},{4,12},{6,14},{8,0},{10,2},{12,4},{14,6},{16,24},{18,... | collective-permute-start | bytes 2359304 | tf_op jit(solution)/shard_map/ppermute | solution.py:938
  117.7 34.1 %collective-permute-start.37 = (bf16[320,1024]{1,0:T(8,128)(2,1)}, bf16[320,1024]{1,0:T(8,128)(2,1)S(1)}, u32[]{:S(2)}, u32[]{:S(2)}) collective-permute-start(bf16[320,1024]{1,0:T(8,128)(2,1)} %get-tuple-element.115), channel_id=1, source_target_pairs={{0,4},{2,6},{4,0},{6,2},{8,12},{10,14},{12,8},{14,10},{16,20},{18,... | collective-permute-start | bytes 1966088 | tf_op jit(solution)/shard_map/ppermute | solution.py:938
  119.8 37.7 %collective-permute-start.44 = (bf16[320,1024]{1,0:T(8,128)(2,1)}, bf16[320,1024]{1,0:T(8,128)(2,1)S(1)}, u32[]{:S(2)}, u32[]{:S(2)}) collective-permute-start(bf16[320,1024]{1,0:T(8,128)(2,1)} %get-tuple-element.121), channel_id=1, source_target_pairs={{0,2},{2,0},{4,6},{6,4},{8,10},{10,8},{12,14},{14,12},{16,18},{18,... | collective-permute-start | bytes 1966088 | tf_op jit(solution)/shard_map/ppermute | solution.py:938
  136.7 33.1 %collective-permute-start.8 = (bf16[768,512]{1,0:T(8,128)(2,1)}, bf16[768,512]{1,0:T(8,128)(2,1)S(1)}, u32[]{:S(2)}, u32[]{:S(2)}) collective-permute-start(bf16[768,512]{1,0:T(8,128)(2,1)} %get-tuple-element.89), channel_id=1, source_target_pairs={{0,8},{2,10},{4,12},{6,14},{8,0},{10,2},{12,4},{14,6},{16,24},{18,... | collective-permute-start | bytes 2359304 | tf_op jit(solution)/shard_map/ppermute | solution.py:938
  138.9 34.9 %collective-permute-start.15 = (bf16[768,512]{1,0:T(8,128)(2,1)S(1)}, bf16[768,512]{1,0:T(8,128)(2,1)S(1)}, u32[]{:S(2)}, u32[]{:S(2)}) collective-permute-start(bf16[768,512]{1,0:T(8,128)(2,1)S(1)} %get-tuple-element.95), channel_id=1, source_target_pairs={{0,2},{2,0},{4,6},{6,4},{8,10},{10,8},{12,14},{14,12},{16,18},{18,... | collective-permute-start | bytes 2359304 | tf_op jit(solution)/shard_map/ppermute | solution.py:938
  157.5 64.0 %collective-permute-start.3 = (bf16[584,1024]{1,0:T(8,128)(2,1)S(1)}, bf16[584,1024]{1,0:T(8,128)(2,1)S(1)}, u32[]{:S(2)}, u32[]{:S(2)}) collective-permute-start(bf16[584,1024]{1,0:T(8,128)(2,1)S(1)} %back_in.1.ga_ref), channel_id=1, source_target_pairs={{0,1},{1,0},{2,3},{3,2},{4,5},{5,4},{6,7},{7,6},{8,9},{9,8},{10,11... | collective-permute-start | bytes 3588104 | tf_op jit(solution)/shard_map/ppermute | solution.py:1005
  173.8 40.7 %collective-permute-start.33 = (bf16[192,1024]{1,0:T(8,128)(2,1)S(1)}, bf16[192,1024]{1,0:T(8,128)(2,1)S(1)}, u32[]{:S(2)}, u32[]{:S(2)}) collective-permute-start(bf16[192,1024]{1,0:T(8,128)(2,1)S(1)} %add.34.refs_1_), channel_id=1, source_target_pairs={{0,2},{2,0},{4,6},{6,4},{8,10},{10,8},{12,14},{14,12},{16,18},{18,... | collective-permute-start | bytes 1179656 | tf_op jit(solution)/shard_map/ppermute | solution.py:946
  177.2 39.4 %collective-permute-start.39 = (bf16[160,1024]{1,0:T(8,128)(2,1)S(1)}, bf16[160,1024]{1,0:T(8,128)(2,1)S(1)}, u32[]{:S(2)}, u32[]{:S(2)}) collective-permute-start(bf16[160,1024]{1,0:T(8,128)(2,1)S(1)} %add.35.a_ref), channel_id=1, source_target_pairs={{0,16},{2,18},{4,20},{6,22},{8,24},{10,26},{12,28},{14,30},{16,0},... | collective-permute-start | bytes 983048 | tf_op jit(solution)/shard_map/ppermute | solution.py:943
  216.6 57.5 %collective-permute-start.34 = (bf16[384,1024]{1,0:T(8,128)(2,1)S(1)}, bf16[384,1024]{1,0:T(8,128)(2,1)S(1)}, u32[]{:S(2)}, u32[]{:S(2)}) collective-permute-start(bf16[384,1024]{1,0:T(8,128)(2,1)S(1)} %join.18.refs_1_), channel_id=1, source_target_pairs={{0,8},{2,10},{4,12},{6,14},{8,0},{10,2},{12,4},{14,6},{16,24},{18,... | collective-permute-start | bytes 2359304 | tf_op jit(solution)/shard_map/ppermute | solution.py:946
  216.8 30.0 %collective-permute-start.40 = (bf16[160,1024]{1,0:T(8,128)(2,1)S(1)}, bf16[160,1024]{1,0:T(8,128)(2,1)S(1)}, u32[]{:S(2)}, u32[]{:S(2)}) collective-permute-start(bf16[160,1024]{1,0:T(8,128)(2,1)S(1)} %add.36.refs_1_), channel_id=1, source_target_pairs={{0,8},{2,10},{4,12},{6,14},{8,0},{10,2},{12,4},{14,6},{16,24},{18,... | collective-permute-start | bytes 983048 | tf_op jit(solution)/shard_map/ppermute | solution.py:946
  220.5 31.2 %collective-permute-start.47 = (bf16[160,1024]{1,0:T(8,128)(2,1)S(1)}, bf16[160,1024]{1,0:T(8,128)(2,1)S(1)}, u32[]{:S(2)}, u32[]{:S(2)}) collective-permute-start(bf16[160,1024]{1,0:T(8,128)(2,1)S(1)} %add.38.refs_1_), channel_id=1, source_target_pairs={{0,4},{2,6},{4,0},{6,2},{8,12},{10,14},{12,8},{14,10},{16,20},{18,... | collective-permute-start | bytes 983048 | tf_op jit(solution)/shard_map/ppermute | solution.py:946
  221.5 33.7 %collective-permute-start.11 = (bf16[192,512]{1,0:T(8,128)(2,1)S(1)}, bf16[192,512]{1,0:T(8,128)(2,1)S(1)}, u32[]{:S(2)}, u32[]{:S(2)}) collective-permute-start(bf16[192,512]{1,0:T(8,128)(2,1)S(1)} %add.27.a_ref), channel_id=1, source_target_pairs={{0,16},{2,18},{4,20},{6,22},{8,24},{10,26},{12,28},{14,30},{16,0},... | collective-permute-start | bytes 589832 | tf_op jit(solution)/shard_map/ppermute | solution.py:943
  251.1 30.9 %collective-permute-start.41 = (bf16[320,1024]{1,0:T(8,128)(2,1)S(1)}, bf16[320,1024]{1,0:T(8,128)(2,1)S(1)}, u32[]{:S(2)}, u32[]{:S(2)}) collective-permute-start(bf16[320,1024]{1,0:T(8,128)(2,1)S(1)} %join.20.refs_1_), channel_id=1, source_target_pairs={{0,4},{2,6},{4,0},{6,2},{8,12},{10,14},{12,8},{14,10},{16,20},{18,... | collective-permute-start | bytes 1966088 | tf_op jit(solution)/shard_map/ppermute | solution.py:946
  254.6 31.8 %collective-permute-start.48 = (bf16[320,1024]{1,0:T(8,128)(2,1)S(1)}, bf16[320,1024]{1,0:T(8,128)(2,1)S(1)}, u32[]{:S(2)}, u32[]{:S(2)}) collective-permute-start(bf16[320,1024]{1,0:T(8,128)(2,1)S(1)} %join.22.refs_1_), channel_id=1, source_target_pairs={{0,2},{2,0},{4,6},{6,4},{8,10},{10,8},{12,14},{14,12},{16,18},{18,... | collective-permute-start | bytes 1966088 | tf_op jit(solution)/shard_map/ppermute | solution.py:946
  280.8 94.6 %collective-permute-start.35 = (bf16[768,1024]{1,0:T(8,128)(2,1)}, bf16[768,1024]{1,0:T(8,128)(2,1)}, u32[]{:S(2)}, u32[]{:S(2)}) collective-permute-start(bf16[768,1024]{1,0:T(8,128)(2,1)} %join.19.own_ref), channel_id=1, source_target_pairs={{0,4},{2,6},{4,0},{6,2},{8,12},{10,14},{12,8},{14,10},{16,20},{18,... | collective-permute-start | bytes 4718600 | tf_op jit(solution)/shard_map/ppermute | solution.py:949
  286.4 50.9 %collective-permute-start.28 = (bf16[256,1024]{1,0:T(8,128)(2,1)S(1)}, bf16[256,1024]{1,0:T(8,128)(2,1)S(1)}, u32[]{:S(2)}, u32[]{:S(2)}) collective-permute-start(bf16[256,1024]{1,0:T(8,128)(2,1)S(1)} %join.17.own_ref), channel_id=1, source_target_pairs={{0,4},{2,6},{4,0},{6,2},{8,12},{10,14},{12,8},{14,10},{16,20},{18,... | collective-permute-start | bytes 1572872 | tf_op jit(solution)/shard_map/ppermute | solution.py:949
  291.0 68.4 %collective-permute-start.49 = (bf16[640,1024]{1,0:T(8,128)(2,1)}, bf16[640,1024]{1,0:T(8,128)(2,1)}, u32[]{:S(2)}, u32[]{:S(2)}) collective-permute-start(bf16[640,1024]{1,0:T(8,128)(2,1)} %join.23.own_ref), channel_id=1, source_target_pairs={{0,8},{2,10},{4,12},{6,14},{8,0},{10,2},{12,4},{14,6},{16,24},{18,... | collective-permute-start | bytes 3932168 | tf_op jit(solution)/shard_map/ppermute | solution.py:949
  291.0 76.4 %collective-permute-start.42 = (bf16[640,1024]{1,0:T(8,128)(2,1)}, bf16[640,1024]{1,0:T(8,128)(2,1)}, u32[]{:S(2)}, u32[]{:S(2)}) collective-permute-start(bf16[640,1024]{1,0:T(8,128)(2,1)} %join.21.own_ref), channel_id=1, source_target_pairs={{0,2},{2,0},{4,6},{6,4},{8,10},{10,8},{12,14},{14,12},{16,18},{18,... | collective-permute-start | bytes 3932168 | tf_op jit(solution)/shard_map/ppermute | solution.py:949
  293.0 38.2 %collective-permute-start.20 = (bf16[384,512]{1,0:T(8,128)(2,1)S(1)}, bf16[384,512]{1,0:T(8,128)(2,1)S(1)}, u32[]{:S(2)}, u32[]{:S(2)}) collective-permute-start(bf16[384,512]{1,0:T(8,128)(2,1)S(1)} %join.14.refs_1_), channel_id=1, source_target_pairs={{0,4},{2,6},{4,0},{6,2},{8,12},{10,14},{12,8},{14,10},{16,20},{18,... | collective-permute-start | bytes 1179656 | tf_op jit(solution)/shard_map/ppermute | solution.py:946
  (62 other events, 524.0 us)
